TPU v7x, 256 devices: a whole 4x4x8 slice. The times are simulated.
256 devices in a mesh: gx: 4 (over z_lo), gy: 8 (over x, core), gz: 8 (over y, z_hi).
Axes of the slice: x: 4, y: 4, z: 8 (z_hi: 2, z_lo: 4; z = z_hi * 4 + z_lo), core: 2. Of those that a mesh axis runs over, the one named last changes fastest.
Arguments:
- vel: float32 [3, 256, 64, 1024], P(None, 'gz', 'gx', 'gy'), may hold values from -6 to 6
- pres: float32 [256, 64, 1024], P('gz', 'gx', 'gy'), may hold values from -6 to 6
- modulus: float32 [256, 64, 1024], P('gz', 'gx', 'gy'), may hold values from 0.05 to 0.5
- adj_vel_in: float32 [3, 256, 64, 1024], P(None, 'gz', 'gx', 'gy'), may hold values from -6 to 6
- adj_pres_in: float32 [256, 64, 1024], P('gz', 'gx', 'gy'), may hold values from -6 to 6
- sensor_values: float32 [8192, 128], P(('gx', 'gy', 'gz')), may hold values from -6 to 6
- sensor_owner: int32 [8192, 1], P(('gx', 'gy', 'gz')), may hold values from 0 to 31; in each aligned block of 32 rows (0 to 31, 32 to 63, ...) at most 4 rows name the same one
- sensor_line: int32 [8192], P(('gx', 'gy', 'gz')), may hold values from 0 to 15
- sensor_step: int32 [8192], P(('gx', 'gy', 'gz')), may hold values from 0 to 1
Outputs:
- adj_vel: float32 [3, 256, 64, 1024], P(None, 'gz', 'gx', 'gy')
- adj_pres: float32 [256, 64, 1024], P('gz', 'gx', 'gy')
- shear_gradient: float32 [256, 64, 1024], P('gz', 'gx', 'gy')
Inputs may be any that keep to these rules, and one draw needn't show every extreme that they name: `sensor_owner`: among the 32 rows of one device at most 4 name the same surface brick, and in every draw some device has 4 rows for one brick.
All inputs are finite; a program needn't handle non-finite values.
Results may differ from a plain program's by a relative error of at most 0.00011.
Values sent between devices are 32-bit elements; how exact they have to be, the bound alone decides.
A program may use at most 64 MiB of HBM per device.

v0:
```python
import jax
import jax.numpy as jnp
from jax import lax
from jax.sharding import PartitionSpec as P

STEPS = 2


def shifted(value, axis, by):
    peers = lax.axis_size(axis)
    pairs = [(i, i + by) for i in range(peers) if 0 <= i + by < peers]
    return lax.ppermute(value, axis, pairs)


def extended(block, sides, width):
    for axis, dim in sides:
        count = lax.axis_size(axis)
        forward = [(i, i + 1) for i in range(count - 1)]
        backward = [(target, source) for source, target in forward]
        low = lax.ppermute(
            lax.slice_in_dim(block, block.shape[dim] - width, None, axis=dim), axis, forward
        )
        high = lax.ppermute(lax.slice_in_dim(block, 0, width, axis=dim), axis, backward)
        block = jnp.concatenate([low, block, high], axis=dim)
    return block


def inner(padded):
    return padded[:, 1:-1, 1:-1, 1:-1]


def laplace(padded):
    center = inner(padded)
    total = padded[:, 2:, 1:-1, 1:-1] + padded[:, :-2, 1:-1, 1:-1]
    total = total + padded[:, 1:-1, 2:, 1:-1] + padded[:, 1:-1, :-2, 1:-1]
    total = total + padded[:, 1:-1, 1:-1, 2:] + padded[:, 1:-1, 1:-1, :-2]
    return total - 6.0 * center


def divergence(padded):
    center = inner(padded)
    along_x = center[0] - padded[0, 1:-1, :-2, 1:-1]
    along_y = center[1] - padded[1, 1:-1, 1:-1, :-2]
    along_z = center[2] - padded[2, :-2, 1:-1, 1:-1]
    return along_x + along_y + along_z


def gradient(field):
    next_x = shifted(field[:, 0:1, :], "gx", -1)
    next_y = shifted(field[:, :, 0:1], "gy", -1)
    next_z = shifted(field[0:1], "gz", -1)
    upper_x = jnp.concatenate([field[:, 1:, :], next_x], axis=1)
    upper_y = jnp.concatenate([field[:, :, 1:], next_y], axis=2)
    upper_z = jnp.concatenate([field[1:], next_z], axis=0)
    return jnp.stack([upper_x - field, upper_y - field, upper_z - field])


def adjoint_halo(stacked):
    return extended(stacked, (("gx", 2), ("gy", 3), ("gz", 1)), 1)


def shards(
    vel,
    pres,
    modulus,
    adj_vel_in,
    adj_pres_in,
    sensor_values,
    sensor_owner,
    sensor_line,
    sensor_step,
):
    owners = lax.axis_size("gx") * lax.axis_size("gy")
    rows = sensor_values.shape[0]
    lines = vel.shape[2]
    code = sensor_step * lines + sensor_line
    owner = sensor_owner[:, 0]
    target = owner * (STEPS * lines) + code
    table = (
        lax.broadcasted_iota(jnp.int32, (owners * STEPS * lines, rows), 0) == target[None, :]
    ).astype(jnp.float32)
    spread = jnp.dot(
        table, sensor_values, precision=lax.Precision.HIGHEST, preferred_element_type=jnp.float32
    )
    forcing = lax.psum_scatter(spread, ("gx", "gy"), scatter_dimension=0, tiled=True)
    forcing = lax.psum(forcing, "gz")
    surface = (lax.axis_index("gz") == 0).astype(jnp.float32)
    forcing = surface * forcing.reshape(STEPS, lines, forcing.shape[1])
    saved = []
    state_v, state_p = (vel, pres)
    for step in range(STEPS):
        padded = extended(state_v, (("gx", 2), ("gy", 3), ("gz", 1)), 1)
        bend = laplace(padded)
        saved.append(bend)
        if step + 1 < STEPS:
            state_p = state_p + 1.0 * divergence(padded)
            state_v = state_v + 0.25 * (gradient(state_p) + modulus[None] * bend)
    lam_v, lam_p = (adj_vel_in, adj_pres_in)
    shear = jnp.zeros(pres.shape, jnp.float32)
    for step in reversed(range(STEPS)):
        lam_v = lam_v.at[2, 0].add(forcing[step])
        both = adjoint_halo(jnp.concatenate([lam_v, modulus[None] * lam_v], axis=0))
        padded = both[:3]
        weighted = laplace(both[3:])
        shear = shear + 0.25 * jnp.sum(lam_v * saved[step], axis=0)
        middle = lam_p - 0.25 * divergence(padded)
        lam_v = lam_v + 0.25 * weighted - 1.0 * gradient(middle)
        lam_p = middle
    return (lam_v, lam_p, shear)


def solution(mesh):
    return jax.shard_map(
        shards,
        mesh=mesh,
        in_specs=(
            P(None, "gz", "gx", "gy"),
            P("gz", "gx", "gy"),
            P("gz", "gx", "gy"),
            P(None, "gz", "gx", "gy"),
            P("gz", "gx", "gy"),
            P(("gx", "gy", "gz"), None),
            P(("gx", "gy", "gz"), None),
            P(("gx", "gy", "gz")),
            P(("gx", "gy", "gz")),
        ),
        out_specs=(P(None, "gz", "gx", "gy"), P("gz", "gx", "gy"), P("gz", "gx", "gy")),
        check_vma=False,
    )
```

profile of v0, /device:TPU:113, one launch (start us, length us, event | category | flops | bytes accessed | tf_op | source)
XLA Modules:
  0.0 409.7 jit_solution(13795292992529190486)
XLA Ops:
  10.7 4.0 collective-permute-start.19
  17.0 120.5 %reduce-scatter.2.cloned.1.call-done = f32[32,128]{1,0:T(8,128)} async-done(((f32[1024,128]{1,0:T(8,128)}), f32[32,128]{1,0:T(8,128)}) %reduce-scatter.2.cloned.1.call-update) | async-done | bytes 16400 | tf_op jit(solution)/shard_map/reduce_scatter | solution.py:85
  137.6 43.1 %psum.7 = f32[32,128]{1,0:T(8,128)S(1)} all-reduce(f32[32,128]{1,0:T(8,128)} %reduce-scatter.2.cloned.1.call-done), channel_id=1, replica_groups=mesh['gx'=4,'gy'=8,'gz'=8] {'gz'}, use_global_device_ids=true, to_apply=%region_1.0 | all-reduce | flops 4096 | bytes 32768 | tf_op jit(solution)/shard_map/psum | solution.py:86
  182.4 4.0 collective-permute-start.1
  189.8 12.2 %collective-permute-start.20 = (f32[3,32,18,1]{1,3,2,0:T(1,128)S(1)}, f32[3,32,18,1]{1,3,2,0:T(1,128)S(1)}, u32[]{:S(2)}, u32[]{:S(2)}) collective-permute-start(f32[3,32,18,1]{1,3,2,0:T(1,128)S(1)} %copy.24), channel_id=1, source_target_pairs={{0,8},{8,16},{16,24},{24,32},{32,40},{40,48},{48,56},{1,9},{9,17},... | collective-permute-start | bytes 20744 | tf_op jit(solution)/shard_map/ppermute | solution.py:20
  210.8 2.9 fusion.65
  216.0 5.6 %collective-permute-start.2 = (f32[6,32,18,1]{1,3,2,0:T(1,128)S(1)}, f32[6,32,18,1]{1,3,2,0:T(1,128)S(1)}, u32[]{:S(2)}, u32[]{:S(2)}) collective-permute-start(f32[6,32,18,1]{1,3,2,0:T(1,128)S(1)} %copy.12), channel_id=1, source_target_pairs={{0,8},{8,16},{16,24},{24,32},{32,40},{40,48},{48,56},{1,9},{9,17},... | collective-permute-start | bytes 41480 | tf_op jit(solution)/shard_map/ppermute | solution.py:20
  227.5 2.9 collective-permute-start.22
  230.4 7.2 %collective-permute-start.26 = (f32[3,1,18,130]{3,2,1,0:T(8,128)}, f32[3,1,18,130]{3,2,1,0:T(8,128)}, u32[]{:S(2)}, u32[]{:S(2)}) collective-permute-start(f32[3,1,18,130]{3,2,1,0:T(8,128)} %get-tuple-element.35), channel_id=1, source_target_pairs={{1,0},{2,1},{3,2},{4,3},{5,4},{6,5},{7,6},{9,8},{10,9},{11,10},{12... | collective-permute-start | bytes 84248 | tf_op jit(solution)/shard_map/ppermute | solution.py:23
  243.6 2.9 collective-permute-start.5
  251.0 7.4 %collective-permute-start.25 = (f32[1,16,128]{2,1,0:T(8,128)S(1)}, f32[1,16,128]{2,1,0:T(8,128)S(1)}, u32[]{:S(2)}, u32[]{:S(2)}) collective-permute-start(f32[1,16,128]{2,1,0:T(8,128)S(1)} %slice.555), channel_id=1, source_target_pairs={{1,0},{2,1},{3,2},{4,3},{5,4},{6,5},{7,6},{9,8},{10,9},{11,10},{12... | collective-permute-start | bytes 24584 | tf_op jit(solution)/shard_map/ppermute | solution.py:12
  260.7 9.7 %collective-permute-start.6 = (f32[32,1,128]{2,1,0:T(1,128)S(1)}, f32[32,1,128]{2,1,0:T(1,128)S(1)}, u32[]{:S(2)}, u32[]{:S(2)}) collective-permute-start(f32[32,1,128]{2,1,0:T(1,128)S(1)} %slice.530), channel_id=1, source_target_pairs={{64,0},{128,64},{192,128},{65,1},{129,65},{193,129},{66,2},{130,66... | collective-permute-start | bytes 49160 | tf_op jit(solution)/shard_map/ppermute | solution.py:12
  270.4 2.9 collective-permute-start.8
  273.6 8.7 %collective-permute-start.4 = (f32[6,1,18,130]{3,2,1,0:T(8,128)S(1)}, f32[6,1,18,130]{3,2,1,0:T(8,128)S(1)}, u32[]{:S(2)}, u32[]{:S(2)}) collective-permute-start(f32[6,1,18,130]{3,2,1,0:T(8,128)S(1)} %get-tuple-element.31), channel_id=1, source_target_pairs={{1,0},{2,1},{3,2},{4,3},{5,4},{6,5},{7,6},{9,8},{10,9},{11,10},{12... | collective-permute-start | bytes 168488 | tf_op jit(solution)/shard_map/ppermute | solution.py:23
  282.6 5.6 %collective-permute-done.4 = f32[6,1,18,130]{3,2,1,0:T(8,128)S(1)} collective-permute-done((f32[6,1,18,130]{3,2,1,0:T(8,128)S(1)}, f32[6,1,18,130]{3,2,1,0:T(8,128)S(1)}, u32[]{:S(2)}, u32[]{:S(2)}) %collective-permute-start.4) | collective-permute-done | bytes 56192 | tf_op jit(solution)/shard_map/ppermute | solution.py:23
  291.1 4.0 multiply_reduce_fusion
  296.7 4.0 collective-permute-start.28
  308.4 5.0 %collective-permute-start.29 = (f32[3,32,18,1]{1,3,2,0:T(1,128)S(1)}, f32[3,32,18,1]{1,3,2,0:T(1,128)S(1)}, u32[]{:S(2)}, u32[]{:S(2)}) collective-permute-start(f32[3,32,18,1]{1,3,2,0:T(1,128)S(1)} %copy.30), channel_id=1, source_target_pairs={{0,8},{8,16},{16,24},{24,32},{32,40},{40,48},{48,56},{1,9},{9,17},... | collective-permute-start | bytes 20744 | tf_op jit(solution)/shard_map/ppermute | solution.py:20
  322.1 2.9 fusion.64
  325.1 3.1 copy.18
  330.1 3.0 copy.19
  333.0 3.0 collective-permute-start.12
  337.7 8.2 %collective-permute-start.31 = (f32[3,1,18,130]{3,2,1,0:T(8,128)}, f32[3,1,18,130]{3,2,1,0:T(8,128)}, u32[]{:S(2)}, u32[]{:S(2)}) collective-permute-start(f32[3,1,18,130]{3,2,1,0:T(8,128)} %get-tuple-element.33), channel_id=1, source_target_pairs={{1,0},{2,1},{3,2},{4,3},{5,4},{6,5},{7,6},{9,8},{10,9},{11,10},{12... | collective-permute-start | bytes 84248 | tf_op jit(solution)/shard_map/ppermute | solution.py:23
  347.9 3.1 copy.20
  351.0 3.1 copy.21
  355.5 6.9 %collective-permute-start.14 = (f32[6,1,18,130]{3,2,1,0:T(8,128)S(1)}, f32[6,1,18,130]{3,2,1,0:T(8,128)S(1)}, u32[]{:S(2)}, u32[]{:S(2)}) collective-permute-start(f32[6,1,18,130]{3,2,1,0:T(8,128)S(1)} %get-tuple-element.30), channel_id=1, source_target_pairs={{0,1},{1,2},{2,3},{3,4},{4,5},{5,6},{6,7},{8,9},{9,10},{10,11},{11... | collective-permute-start | bytes 168488 | tf_op jit(solution)/shard_map/ppermute | solution.py:20
  364.7 3.5 collective-permute-done.14
  371.1 7.2 %collective-permute-start.15 = (f32[32,1,128]{2,1,0:T(1,128)S(1)}, f32[32,1,128]{2,1,0:T(1,128)S(1)}, u32[]{:S(2)}, u32[]{:S(2)}) collective-permute-start(f32[32,1,128]{2,1,0:T(1,128)S(1)} %slice.543), channel_id=1, source_target_pairs={{64,0},{128,64},{192,128},{65,1},{129,65},{193,129},{66,2},{130,66... | collective-permute-start | bytes 49160 | tf_op jit(solution)/shard_map/ppermute | solution.py:12
  378.3 6.2 %collective-permute-start.17 = (f32[1,16,128]{2,1,0:T(8,128)S(1)}, f32[1,16,128]{2,1,0:T(8,128)S(1)}, u32[]{:S(2)}, u32[]{:S(2)}) collective-permute-start(f32[1,16,128]{2,1,0:T(8,128)S(1)} %slice.547), channel_id=1, source_target_pairs={{1,0},{2,1},{3,2},{4,3},{5,4},{6,5},{7,6},{9,8},{10,9},{11,10},{12... | collective-permute-start | bytes 24584 | tf_op jit(solution)/shard_map/ppermute | solution.py:12
  385.3 3.8 collective-permute-start.13
  389.5 9.9 %collective-permute-done.13 = f32[6,1,18,130]{3,2,1,0:T(8,128)S(1)} collective-permute-done((f32[6,1,18,130]{3,2,1,0:T(8,128)S(1)}, f32[6,1,18,130]{3,2,1,0:T(8,128)S(1)}, u32[]{:S(2)}, u32[]{:S(2)}) %collective-permute-start.13) | collective-permute-done | bytes 56192 | tf_op jit(solution)/shard_map/ppermute | solution.py:23
  399.4 3.4 fusion.17
  (171 shorter events, 74.5 us)
Async XLA Ops:
  7.2 130.4 %reduce-scatter.2.cloned.1.call-start = ((), (), s32[]{:S(2)}) async-start(), calls=%async_computation.1 | async-start | bytes 540672 | tf_op jit(solution)/shard_map/reduce_scatter | solution.py:85
  9.4 5.3 %collective-permute-start.18 = (f32[3,32,1,128]{3,2,1,0:T(1,128)S(1)}, f32[3,32,1,128]{3,2,1,0:T(1,128)S(1)}, u32[]{:S(2)}, u32[]{:S(2)}) collective-permute-start(f32[3,32,1,128]{3,2,1,0:T(1,128)S(1)} %get-tuple-element.51), channel_id=1, source_target_pairs={{0,64},{64,128},{128,192},{1,65},{65,129},{129,193},{2,66},{66,130... | collective-permute-start | bytes 147464 | tf_op jit(solution)/shard_map/ppermute | solution.py:20
  181.0 29.4 %collective-permute-start = (f32[6,32,1,128]{3,2,1,0:T(1,128)S(1)}, f32[6,32,1,128]{3,2,1,0:T(1,128)S(1)}, u32[]{:S(2)}, u32[]{:S(2)}) collective-permute-start(f32[6,32,1,128]{3,2,1,0:T(1,128)S(1)} %get-tuple-element.43), channel_id=1, source_target_pairs={{0,64},{64,128},{128,192},{1,65},{65,129},{129,193},{2,66},{66,130... | collective-permute-start | bytes 294920 | tf_op jit(solution)/shard_map/ppermute | solution.py:20
  182.4 28.0 %collective-permute-start.1 = (f32[6,32,1,128]{3,2,1,0:T(1,128)S(1)}, f32[6,32,1,128]{3,2,1,0:T(1,128)S(1)}, u32[]{:S(2)}, u32[]{:S(2)}) collective-permute-start(f32[6,32,1,128]{3,2,1,0:T(1,128)S(1)} %get-tuple-element.44), channel_id=1, source_target_pairs={{64,0},{128,64},{192,128},{65,1},{129,65},{193,129},{66,2},{130,66... | collective-permute-start | bytes 294920 | tf_op jit(solution)/shard_map/ppermute | solution.py:23
  189.8 15.8 %collective-permute-start.20 = (f32[3,32,18,1]{1,3,2,0:T(1,128)S(1)}, f32[3,32,18,1]{1,3,2,0:T(1,128)S(1)}, u32[]{:S(2)}, u32[]{:S(2)}) collective-permute-start(f32[3,32,18,1]{1,3,2,0:T(1,128)S(1)} %copy.24), channel_id=1, source_target_pairs={{0,8},{8,16},{16,24},{24,32},{32,40},{40,48},{48,56},{1,9},{9,17},... | collective-permute-start | bytes 20744 | tf_op jit(solution)/shard_map/ppermute | solution.py:20
  203.7 5.2 %collective-permute-start.21 = (f32[3,32,18,1]{1,3,2,0:T(1,128)S(1)}, f32[3,32,18,1]{1,3,2,0:T(1,128)S(1)}, u32[]{:S(2)}, u32[]{:S(2)}) collective-permute-start(f32[3,32,18,1]{1,3,2,0:T(1,128)S(1)} %copy.26), channel_id=1, source_target_pairs={{8,0},{16,8},{24,16},{32,24},{40,32},{48,40},{56,48},{9,1},{17,9},... | collective-permute-start | bytes 20744 | tf_op jit(solution)/shard_map/ppermute | solution.py:23
  216.0 21.6 %collective-permute-start.2 = (f32[6,32,18,1]{1,3,2,0:T(1,128)S(1)}, f32[6,32,18,1]{1,3,2,0:T(1,128)S(1)}, u32[]{:S(2)}, u32[]{:S(2)}) collective-permute-start(f32[6,32,18,1]{1,3,2,0:T(1,128)S(1)} %copy.12), channel_id=1, source_target_pairs={{0,8},{8,16},{16,24},{24,32},{32,40},{40,48},{48,56},{1,9},{9,17},... | collective-permute-start | bytes 41480 | tf_op jit(solution)/shard_map/ppermute | solution.py:20
  224.0 15.9 %collective-permute-start.3 = (f32[6,32,18,1]{1,3,2,0:T(1,128)S(1)}, f32[6,32,18,1]{1,3,2,0:T(1,128)S(1)}, u32[]{:S(2)}, u32[]{:S(2)}) collective-permute-start(f32[6,32,18,1]{1,3,2,0:T(1,128)S(1)} %copy.13), channel_id=1, source_target_pairs={{8,0},{16,8},{24,16},{32,24},{40,32},{48,40},{56,48},{9,1},{17,9},... | collective-permute-start | bytes 41480 | tf_op jit(solution)/shard_map/ppermute | solution.py:23
  227.5 19.0 %collective-permute-start.22 = (f32[3,1,18,130]{3,2,1,0:T(8,128)S(1)}, f32[3,1,18,130]{3,2,1,0:T(8,128)S(1)}, u32[]{:S(2)}, u32[]{:S(2)}) collective-permute-start(f32[3,1,18,130]{3,2,1,0:T(8,128)S(1)} %get-tuple-element.36), channel_id=1, source_target_pairs={{0,1},{1,2},{2,3},{3,4},{4,5},{5,6},{6,7},{8,9},{9,10},{10,11},{11... | collective-permute-start | bytes 84248 | tf_op jit(solution)/shard_map/ppermute | solution.py:20
  230.4 60.6 %collective-permute-start.26 = (f32[3,1,18,130]{3,2,1,0:T(8,128)}, f32[3,1,18,130]{3,2,1,0:T(8,128)}, u32[]{:S(2)}, u32[]{:S(2)}) collective-permute-start(f32[3,1,18,130]{3,2,1,0:T(8,128)} %get-tuple-element.35), channel_id=1, source_target_pairs={{1,0},{2,1},{3,2},{4,3},{5,4},{6,5},{7,6},{9,8},{10,9},{11,10},{12... | collective-permute-start | bytes 84248 | tf_op jit(solution)/shard_map/ppermute | solution.py:23
  243.6 14.8 %collective-permute-start.5 = (f32[6,1,18,130]{3,2,1,0:T(8,128)S(1)}, f32[6,1,18,130]{3,2,1,0:T(8,128)S(1)}, u32[]{:S(2)}, u32[]{:S(2)}) collective-permute-start(f32[6,1,18,130]{3,2,1,0:T(8,128)S(1)} %get-tuple-element.32), channel_id=1, source_target_pairs={{0,1},{1,2},{2,3},{3,4},{4,5},{5,6},{6,7},{8,9},{9,10},{10,11},{11... | collective-permute-start | bytes 168488 | tf_op jit(solution)/shard_map/ppermute | solution.py:20
  247.4 13.3 %collective-permute-start.24 = (f32[32,16,1]{2,1,0:T(8,128)S(1)}, f32[32,16,1]{2,1,0:T(8,128)S(1)}, u32[]{:S(2)}, u32[]{:S(2)}) collective-permute-start(f32[32,16,1]{2,1,0:T(8,128)S(1)} %bitcast.50), channel_id=1, source_target_pairs={{8,0},{16,8},{24,16},{32,24},{40,32},{48,40},{56,48},{9,1},{17,9},... | collective-permute-start | bytes 6152 | tf_op jit(solution)/shard_map/ppermute | solution.py:12
  249.3 24.1 %collective-permute-start.23 = (f32[32,1,128]{2,1,0:T(1,128)S(1)}, f32[32,1,128]{2,1,0:T(1,128)S(1)}, u32[]{:S(2)}, u32[]{:S(2)}) collective-permute-start(f32[32,1,128]{2,1,0:T(1,128)S(1)} %slice.551), channel_id=1, source_target_pairs={{64,0},{128,64},{192,128},{65,1},{129,65},{193,129},{66,2},{130,66... | collective-permute-start | bytes 49160 | tf_op jit(solution)/shard_map/ppermute | solution.py:12
  251.0 19.5 %collective-permute-start.25 = (f32[1,16,128]{2,1,0:T(8,128)S(1)}, f32[1,16,128]{2,1,0:T(8,128)S(1)}, u32[]{:S(2)}, u32[]{:S(2)}) collective-permute-start(f32[1,16,128]{2,1,0:T(8,128)S(1)} %slice.555), channel_id=1, source_target_pairs={{1,0},{2,1},{3,2},{4,3},{5,4},{6,5},{7,6},{9,8},{10,9},{11,10},{12... | collective-permute-start | bytes 24584 | tf_op jit(solution)/shard_map/ppermute | solution.py:12
  258.8 23.7 %collective-permute-start.7 = (f32[32,16,1]{2,1,0:T(8,128)S(1)}, f32[32,16,1]{2,1,0:T(8,128)S(1)}, u32[]{:S(2)}, u32[]{:S(2)}) collective-permute-start(f32[32,16,1]{2,1,0:T(8,128)S(1)} %bitcast.48), channel_id=1, source_target_pairs={{8,0},{16,8},{24,16},{32,24},{40,32},{48,40},{56,48},{9,1},{17,9},... | collective-permute-start | bytes 6152 | tf_op jit(solution)/shard_map/ppermute | solution.py:12
  260.7 21.7 %collective-permute-start.6 = (f32[32,1,128]{2,1,0:T(1,128)S(1)}, f32[32,1,128]{2,1,0:T(1,128)S(1)}, u32[]{:S(2)}, u32[]{:S(2)}) collective-permute-start(f32[32,1,128]{2,1,0:T(1,128)S(1)} %slice.530), channel_id=1, source_target_pairs={{64,0},{128,64},{192,128},{65,1},{129,65},{193,129},{66,2},{130,66... | collective-permute-start | bytes 49160 | tf_op jit(solution)/shard_map/ppermute | solution.py:12
  270.4 12.0 %collective-permute-start.8 = (f32[1,16,128]{2,1,0:T(8,128)S(1)}, f32[1,16,128]{2,1,0:T(8,128)S(1)}, u32[]{:S(2)}, u32[]{:S(2)}) collective-permute-start(f32[1,16,128]{2,1,0:T(8,128)S(1)} %slice.534), channel_id=1, source_target_pairs={{1,0},{2,1},{3,2},{4,3},{5,4},{6,5},{7,6},{9,8},{10,9},{11,10},{12... | collective-permute-start | bytes 24584 | tf_op jit(solution)/shard_map/ppermute | solution.py:12
  273.6 14.7 %collective-permute-start.4 = (f32[6,1,18,130]{3,2,1,0:T(8,128)S(1)}, f32[6,1,18,130]{3,2,1,0:T(8,128)S(1)}, u32[]{:S(2)}, u32[]{:S(2)}) collective-permute-start(f32[6,1,18,130]{3,2,1,0:T(8,128)S(1)} %get-tuple-element.31), channel_id=1, source_target_pairs={{1,0},{2,1},{3,2},{4,3},{5,4},{6,5},{7,6},{9,8},{10,9},{11,10},{12... | collective-permute-start | bytes 168488 | tf_op jit(solution)/shard_map/ppermute | solution.py:23
  295.4 9.3 %collective-permute-start.27 = (f32[3,32,1,128]{3,2,1,0:T(1,128)S(1)}, f32[3,32,1,128]{3,2,1,0:T(1,128)S(1)}, u32[]{:S(2)}, u32[]{:S(2)}) collective-permute-start(f32[3,32,1,128]{3,2,1,0:T(1,128)S(1)} %get-tuple-element.49), channel_id=1, source_target_pairs={{0,64},{64,128},{128,192},{1,65},{65,129},{129,193},{2,66},{66,130... | collective-permute-start | bytes 147464 | tf_op jit(solution)/shard_map/ppermute | solution.py:20
  296.7 8.1 %collective-permute-start.28 = (f32[3,32,1,128]{3,2,1,0:T(1,128)S(1)}, f32[3,32,1,128]{3,2,1,0:T(1,128)S(1)}, u32[]{:S(2)}, u32[]{:S(2)}) collective-permute-start(f32[3,32,1,128]{3,2,1,0:T(1,128)S(1)} %get-tuple-element.50), channel_id=1, source_target_pairs={{64,0},{128,64},{192,128},{65,1},{129,65},{193,129},{66,2},{130,66... | collective-permute-start | bytes 147464 | tf_op jit(solution)/shard_map/ppermute | solution.py:23
  300.9 20.9 %collective-permute-start.10 = (f32[6,32,1,128]{3,2,1,0:T(1,128)S(1)}, f32[6,32,1,128]{3,2,1,0:T(1,128)S(1)}, u32[]{:S(2)}, u32[]{:S(2)}) collective-permute-start(f32[6,32,1,128]{3,2,1,0:T(1,128)S(1)} %get-tuple-element.42), channel_id=1, source_target_pairs={{64,0},{128,64},{192,128},{65,1},{129,65},{193,129},{66,2},{130,66... | collective-permute-start | bytes 294920 | tf_op jit(solution)/shard_map/ppermute | solution.py:23
  303.4 18.3 %collective-permute-start.9 = (f32[6,32,1,128]{3,2,1,0:T(1,128)S(1)}, f32[6,32,1,128]{3,2,1,0:T(1,128)S(1)}, u32[]{:S(2)}, u32[]{:S(2)}) collective-permute-start(f32[6,32,1,128]{3,2,1,0:T(1,128)S(1)} %get-tuple-element.41), channel_id=1, source_target_pairs={{0,64},{64,128},{128,192},{1,65},{65,129},{129,193},{2,66},{66,130... | collective-permute-start | bytes 294920 | tf_op jit(solution)/shard_map/ppermute | solution.py:20
  308.4 8.6 %collective-permute-start.29 = (f32[3,32,18,1]{1,3,2,0:T(1,128)S(1)}, f32[3,32,18,1]{1,3,2,0:T(1,128)S(1)}, u32[]{:S(2)}, u32[]{:S(2)}) collective-permute-start(f32[3,32,18,1]{1,3,2,0:T(1,128)S(1)} %copy.30), channel_id=1, source_target_pairs={{0,8},{8,16},{16,24},{24,32},{32,40},{40,48},{48,56},{1,9},{9,17},... | collective-permute-start | bytes 20744 | tf_op jit(solution)/shard_map/ppermute | solution.py:20
  328.1 19.7 %collective-permute-start.11 = (f32[6,32,18,1]{1,3,2,0:T(1,128)}, f32[6,32,18,1]{1,3,2,0:T(1,128)}, u32[]{:S(2)}, u32[]{:S(2)}) collective-permute-start(f32[6,32,18,1]{1,3,2,0:T(1,128)} %copy.18), channel_id=1, source_target_pairs={{0,8},{8,16},{16,24},{24,32},{32,40},{40,48},{48,56},{1,9},{9,17},... | collective-permute-start | bytes 41480 | tf_op jit(solution)/shard_map/ppermute | solution.py:20
  333.0 18.0 %collective-permute-start.12 = (f32[6,32,18,1]{1,3,2,0:T(1,128)}, f32[6,32,18,1]{1,3,2,0:T(1,128)}, u32[]{:S(2)}, u32[]{:S(2)}) collective-permute-start(f32[6,32,18,1]{1,3,2,0:T(1,128)} %copy.19), channel_id=1, source_target_pairs={{8,0},{16,8},{24,16},{32,24},{40,32},{48,40},{56,48},{9,1},{17,9},... | collective-permute-start | bytes 41480 | tf_op jit(solution)/shard_map/ppermute | solution.py:23
  337.7 24.7 %collective-permute-start.31 = (f32[3,1,18,130]{3,2,1,0:T(8,128)}, f32[3,1,18,130]{3,2,1,0:T(8,128)}, u32[]{:S(2)}, u32[]{:S(2)}) collective-permute-start(f32[3,1,18,130]{3,2,1,0:T(8,128)} %get-tuple-element.33), channel_id=1, source_target_pairs={{1,0},{2,1},{3,2},{4,3},{5,4},{6,5},{7,6},{9,8},{10,9},{11,10},{12... | collective-permute-start | bytes 84248 | tf_op jit(solution)/shard_map/ppermute | solution.py:23
  346.0 16.5 %collective-permute-start.32 = (f32[3,1,18,130]{3,2,1,0:T(8,128)}, f32[3,1,18,130]{3,2,1,0:T(8,128)}, u32[]{:S(2)}, u32[]{:S(2)}) collective-permute-start(f32[3,1,18,130]{3,2,1,0:T(8,128)} %get-tuple-element.34), channel_id=1, source_target_pairs={{0,1},{1,2},{2,3},{3,4},{4,5},{5,6},{6,7},{8,9},{9,10},{10,11},{11... | collective-permute-start | bytes 84248 | tf_op jit(solution)/shard_map/ppermute | solution.py:20
  355.5 12.7 %collective-permute-start.14 = (f32[6,1,18,130]{3,2,1,0:T(8,128)S(1)}, f32[6,1,18,130]{3,2,1,0:T(8,128)S(1)}, u32[]{:S(2)}, u32[]{:S(2)}) collective-permute-start(f32[6,1,18,130]{3,2,1,0:T(8,128)S(1)} %get-tuple-element.30), channel_id=1, source_target_pairs={{0,1},{1,2},{2,3},{3,4},{4,5},{5,6},{6,7},{8,9},{9,10},{10,11},{11... | collective-permute-start | bytes 168488 | tf_op jit(solution)/shard_map/ppermute | solution.py:20
  368.5 20.8 %collective-permute-start.16 = (f32[32,16,1]{2,1,0:T(8,128)S(1)}, f32[32,16,1]{2,1,0:T(8,128)S(1)}, u32[]{:S(2)}, u32[]{:S(2)}) collective-permute-start(f32[32,16,1]{2,1,0:T(8,128)S(1)} %bitcast.49), channel_id=1, source_target_pairs={{8,0},{16,8},{24,16},{32,24},{40,32},{48,40},{56,48},{9,1},{17,9},... | collective-permute-start | bytes 6152 | tf_op jit(solution)/shard_map/ppermute | solution.py:12
  371.1 18.3 %collective-permute-start.15 = (f32[32,1,128]{2,1,0:T(1,128)S(1)}, f32[32,1,128]{2,1,0:T(1,128)S(1)}, u32[]{:S(2)}, u32[]{:S(2)}) collective-permute-start(f32[32,1,128]{2,1,0:T(1,128)S(1)} %slice.543), channel_id=1, source_target_pairs={{64,0},{128,64},{192,128},{65,1},{129,65},{193,129},{66,2},{130,66... | collective-permute-start | bytes 49160 | tf_op jit(solution)/shard_map/ppermute | solution.py:12
  378.3 11.0 %collective-permute-start.17 = (f32[1,16,128]{2,1,0:T(8,128)S(1)}, f32[1,16,128]{2,1,0:T(8,128)S(1)}, u32[]{:S(2)}, u32[]{:S(2)}) collective-permute-start(f32[1,16,128]{2,1,0:T(8,128)S(1)} %slice.547), channel_id=1, source_target_pairs={{1,0},{2,1},{3,2},{4,3},{5,4},{6,5},{7,6},{9,8},{10,9},{11,10},{12... | collective-permute-start | bytes 24584 | tf_op jit(solution)/shard_map/ppermute | solution.py:12
  385.3 14.1 %collective-permute-start.13 = (f32[6,1,18,130]{3,2,1,0:T(8,128)S(1)}, f32[6,1,18,130]{3,2,1,0:T(8,128)S(1)}, u32[]{:S(2)}, u32[]{:S(2)}) collective-permute-start(f32[6,1,18,130]{3,2,1,0:T(8,128)S(1)} %get-tuple-element.29), channel_id=1, source_target_pairs={{1,0},{2,1},{3,2},{4,3},{5,4},{6,5},{7,6},{9,8},{10,9},{11,10},{12... | collective-permute-start | bytes 168488 | tf_op jit(solution)/shard_map/ppermute | solution.py:23
  (36 other events, 1119.1 us)
Sparse Core Ops, SparseCore 0:
  11.1 126.4 reduce-scatter.1
where the time goes:
time: 411 us; the launch traced here: 410 us
  waiting for transfers between devices  144 us (35%)
  starting transfers between devices  137 us (33%)
  local copies, waits for them, and re-layouts  44.7 us (11%)
  blocking collectives  43.1 us (10%)
  other arithmetic  24 us (6%)
  between operations  15.1 us (4%)
    reduce_scatter x1, waiting for transfers between devices, shards(): lax.psum_scatter(spread, ('gx', 'gy'), scatter_dimension=0, tiled=True)  121 us
    ppermute x12, starting transfers between devices, extended(): lax.ppermute(lax.slice_in_dim(block, 0, width, axis=dim), axis, backward)  51.2 us
    ppermute x12, starting transfers between devices, extended(): lax.ppermute(lax.slice_in_dim(block, block.shape[dim] - width, None, axis...  44.7 us
    psum x1, blocking collectives, shards(): forcing = lax.psum(forcing, 'gz')  43.1 us
    ppermute x9, starting transfers between devices, shifted(): return lax.ppermute(value, axis, pairs)  41.5 us
    ppermute x12, waiting for transfers between devices, extended(): lax.ppermute(lax.slice_in_dim(block, 0, width, axis=dim), axis, backward)  20.1 us
    slice x7, local copies, waits for them, and re-layouts, extended(): lax.slice_in_dim(block, 0, width, axis=dim)  16.2 us
    slice x7, local copies, waits for them, and re-layouts, extended(): lax.slice_in_dim(block, block.shape[dim] - width, None, axis=dim)  10.7 us
  transfers between devices with their start and end apart: 34, of which 7 were waited for; matrix products, arithmetic and copies ran while one was open for 12% of the time, Pallas kernels for 0%

commit v1 on v0

v1 whole, which is shorter than its diff:
```python
import jax
import jax.numpy as jnp
from jax import lax
from jax.experimental import pallas as pl
from jax.experimental.pallas import tpu as pltpu
from jax.sharding import PartitionSpec as P

MESH = pl.DeviceIdType.MESH
F32 = jnp.float32
CZ, CX, CY = 32, 16, 128
PITCH = 32
LAYERS = CZ + 2
ROWS = LAYERS * PITCH
NGX, NGY, NGZ = 4, 8, 8
HIGH = lax.Precision.HIGHEST


def body(
    vel, pres, modulus, avel, apres, svals, sowner, sline, sstep,
    o_av, o_ap, o_sh,
    v0, a1, ma, md, p1, m1, v1, a0, ma0, m0,
    p0, ap, bend0, lm, lm0, sh, out,
    ys1, yl1, yh1, ys2, yh2, ys3, yl3, yh3, ys4, yh4,
    ys5, yl5, yh5, ys6, yh6, ys7, yl7, yh7, ys8, yh8,
    xa1, xb1, xh1, xl1, xa2, xh2, xa3, xb3, xh3, xl3, xa4, xh4,
    xa5, xb5, xh5, xl5, xa6, xh6, xa7, xb7, xh7, xl7, xa8, xh8,
    zl, zu, cs, gath, dense, hsum, esum, ksum,
    in_sem, out_sem, xs_sem, xr_sem, ys_sem, yr_sem, zs_sem, zr_sem,
    f1s, f1r, f2s, f2r, f3s, f3r,
):
    gx, gy, gz = lax.axis_index("gx"), lax.axis_index("gy"), lax.axis_index("gz")
    has_xm, has_xp = gx > 0, gx < NGX - 1
    has_ym, has_yp = gy > 0, gy < NGY - 1
    has_zm, has_zp = gz > 0, gz < NGZ - 1
    barrier = pltpu.get_barrier_semaphore()

    def grid3(ref):
        if len(ref.shape) == 3:
            return ref.reshape(3, LAYERS, PITCH, CY).at[:, pl.ds(1, CZ), pl.ds(8, CX), :]
        return ref.reshape(LAYERS, PITCH, CY).at[pl.ds(1, CZ), pl.ds(8, CX), :]

    loads = [
        pltpu.make_async_copy(src, dst, in_sem.at[i])
        for i, (src, dst) in enumerate(
            [(avel, grid3(a1)), (modulus, grid3(md)), (vel, grid3(v0)), (pres, p0), (apres, ap)]
        )
    ]
    for copy in loads:
        copy.start()

    lane = lax.broadcasted_iota(jnp.int32, (CX, CY), 1)

    @pl.when(jnp.logical_not(has_ym))
    def _():
        for ref in (yl1, yl3, yl7):
            ref[...] = jnp.zeros(ref.shape, F32)
        yl5[...] = jnp.zeros(yl5.shape, F32)

    @pl.when(jnp.logical_not(has_yp))
    def _():
        for ref in (yh1, yh2, yh3, yh4, yh6, yh7, yh8):
            ref[...] = jnp.zeros(ref.shape, F32)
        yh5[...] = jnp.zeros(yh5.shape, F32)

    def greet(device):
        pl.semaphore_signal(barrier, inc=1, device_id=device, device_id_type=MESH)

    @pl.when(has_zm)
    def _():
        greet((gx, gy, gz - 1))

    @pl.when(has_zp)
    def _():
        greet((gx, gy, gz + 1))

    @pl.when(gz == 0)
    def _():
        for other in range(2, NGZ):
            greet((gx, gy, other))

    for step in range(1, NGY):
        greet((gx, lax.rem(gy + step, NGY), gz))
    for step in range(1, NGX):
        greet((lax.rem(gx + step, NGX), gy, gz))
    expected = (
        NGX - 1 + NGY - 1
        + has_zm.astype(jnp.int32) + has_zp.astype(jnp.int32) + (gz >= 2).astype(jnp.int32)
    )

    def comps(ref):
        return [ref.at[c] for c in range(3)]

    V0, A1, MA, V1, A0, MA0 = (comps(r) for r in (v0, a1, ma, v1, a0, ma0))

    zeros_layer = jnp.zeros((PITCH, CY), F32)
    zeros_rows = jnp.zeros((LAYERS, CY), F32)
    for ref in V0 + A1 + MA + V1 + A0 + MA0 + [p1, m1, m0]:
        ref[0:PITCH, :] = zeros_layer
        ref[ROWS - PITCH:ROWS, :] = zeros_layer

    @pl.when(jnp.logical_not(has_xm))
    def _():
        for ref in V0 + [A1[0]] + MA + V1 + [A0[0]] + MA0:
            ref[pl.ds(7, LAYERS, stride=PITCH), :] = zeros_rows

    @pl.when(jnp.logical_not(has_xp))
    def _():
        for ref in V0 + MA + [A1[2]] + V1 + MA0 + [p1, m1, m0]:
            ref[pl.ds(24, LAYERS, stride=PITCH), :] = zeros_rows

    owner_col = sowner[...].astype(F32)
    r0 = lax.broadcasted_iota(jnp.int32, (32, 32), 0)
    r1 = lax.broadcasted_iota(jnp.int32, (32, 32), 1)
    owner_row = jnp.sum(jnp.where(r0 == r1, owner_col, 0.0), axis=0, keepdims=True)
    rank = jnp.sum(
        jnp.where((owner_col == owner_row) & (r0 < r1), 1.0, 0.0), axis=0, keepdims=True
    ).astype(jnp.int32)
    owner_int = owner_row.astype(jnp.int32)
    own_gx, own_gy = owner_int >> 3, owner_int & 7
    place = own_gy * 32 + own_gx * 8 + rank
    code_row = (own_gx * 32 + sstep[...] * CX + sline[...] + 1).astype(F32)
    code_col = jnp.sum(jnp.where(r0 == r1, code_row, 0.0), axis=1, keepdims=True)
    slot = lax.broadcasted_iota(jnp.int32, (256, 32), 0)
    cs[...] = jnp.dot(
        (slot == place).astype(F32), svals[...], precision=HIGH, preferred_element_type=F32
    ) + jnp.dot(
        (slot == place + 4).astype(F32), jnp.broadcast_to(code_col, (32, CY)),
        precision=HIGH, preferred_element_type=F32,
    )
    mine = pl.ds(pl.multiple_of(gy * 32, 32), 32)
    gath[mine, :] = cs[mine, :]

    def ld(ref, z, dx=0):
        return ref[pl.ds((z + 1) * PITCH + 8 + dx, CX), :]

    def st(ref, z, value):
        ref[pl.ds(pl.multiple_of((z + 1) * PITCH + 8, 8), CX), :] = value

    def ylo(u, blk, z, f):
        shift = (CY - ((z >> 2) * 16 + 2 * f)) & (CY - 1)
        return jnp.where(lane == 0, pltpu.roll(blk[z & 3], shift, 1), pltpu.roll(u, 1, 1))

    def yhi(u, blk, z, f):
        shift = CY - 2 - (z >> 2) * 16 - 2 * f
        return jnp.where(lane == CY - 1, pltpu.roll(blk[z & 3], shift, 1), pltpu.roll(u, CY - 1, 1))

    def lap(ref, z, yl, yh, f):
        c = ld(ref, z)
        total = ld(ref, z, 1) + ld(ref, z, -1) + (ld(ref, z + 1) + ld(ref, z - 1))
        return total + (ylo(c, yl, z, f) + yhi(c, yh, z, f)) - 6.0 * c

    def div(refs, z, yl, f):
        x, y, w = (ld(r, z) for r in refs)
        return (x - ld(refs[0], z, -1)) + (y - ylo(y, yl, z, f)) + (w - ld(refs[2], z - 1))

    def grad(ref, z, yh, f):
        q = ld(ref, z)
        return ld(ref, z, 1) - q, yhi(q, yh, z, f) - q, ld(ref, z + 1) - q

    def s1(z, yl, yh):
        for c in range(3):
            bend0[c, z] = lap(V0[c], z, yl, yh, c)
            lm[c, z] = lap(MA[c], z, yl, yh, 3 + c)
        st(p1, z, p0[z] + div(V0, z, yl, 1))
        st(m1, z, ap[z] - 0.25 * div(A1, z, yl, 6))

    def s2(z, yh):
        gp, gm = grad(p1, z, yh, 0), grad(m1, z, yh, 1)
        g = ld(md, z)
        for c in range(3):
            st(V1[c], z, ld(V0[c], z) + 0.25 * (gp[c] + g * bend0[c, z]))
            new = ld(A1[c], z) + 0.25 * lm[c, z] - gm[c]
            st(A0[c], z, new)
            st(MA0[c], z, g * new)

    def s3(z, yl, yh):
        total = None
        for c in range(3):
            part = ld(A1[c], z) * lap(V1[c], z, yl, yh, c) + ld(A0[c], z) * bend0[c, z]
            total = part if total is None else total + part
            lm0[c, z] = lap(MA0[c], z, yl, yh, 3 + c)
        sh[z] = 0.25 * total
        st(m0, z, ld(m1, z) - 0.25 * div(A0, z, yl, 6))

    def s4(z, yh):
        gm = grad(m0, z, yh, 0)
        for c in range(3):
            out[c, z] = ld(A0[c], z) + 0.25 * lm0[c, z] - gm[c]

    def every(fn, unroll=1):
        def step(z, carry):
            fn(z)
            return carry
        lax.fori_loop(0, CZ, step, 0, unroll=unroll)

    def pack_y(dst, fields, last=None):
        def step(zz, carry):
            acc = jnp.zeros((CX, CY), F32)
            for g in range(8):
                for f, ref in enumerate(fields):
                    s = g * 16 + 2 * f + 1
                    acc = jnp.where((lane >> 1) == (s >> 1), pltpu.roll(ld(ref, g * 4 + zz), s, 1), acc)
            dst[zz] = acc
            return carry
        lax.fori_loop(0, 4, step, 0)
        if last is not None:
            dst[3] = jnp.where(lane >= CY - 2, pltpu.roll(ld(last, CZ), CY - 1, 1), dst[3])

    def face(ref, x):
        return ref[pl.ds(PITCH + 8 + x, CZ, stride=PITCH), :]

    def pack_x(dst, fields, x):
        for i, ref in enumerate(fields):
            dst[i * CZ:(i + 1) * CZ, :] = face(ref, x)

    def unpack_x(src, fields, x):
        for i, ref in enumerate(fields):
            ref[pl.ds(PITCH + 8 + x, CZ, stride=PITCH), :] = src[i * CZ:(i + 1) * CZ, :]

    def rows_of(pairs, x):
        return [(ref, (z + 1) * PITCH + 8 + x) for ref, z in pairs]

    def pack_rows(dst, pairs, x):
        for i, (ref, row) in enumerate(rows_of(pairs, x)):
            dst[i:i + 1, :] = ref[row:row + 1, :]

    def unpack_rows(src, pairs, x):
        for i, (ref, row) in enumerate(rows_of(pairs, x)):
            ref[row:row + 1, :] = src[i:i + 1, :]

    class Link:
        def __init__(self, src, dst, send, recv, device, sends, gets):
            self.copy = pltpu.make_async_remote_copy(
                src_ref=src, dst_ref=dst, send_sem=send, recv_sem=recv,
                device_id=device, device_id_type=MESH,
            )
            self.sends, self.gets = sends, gets

        def start(self):
            pl.when(self.sends)(self.copy.start)

        def arrive(self):
            pl.when(self.gets)(self.copy.wait_recv)

        def flush(self):
            pl.when(self.sends)(self.copy.wait_send)

    links = []
    counts = {"x": 0, "y": 0, "z": 0}

    def link(kind, src, dst, device, sends, gets):
        n = counts[kind]
        counts[kind] += 1
        ss, rs = {"x": (xs_sem, xr_sem), "y": (ys_sem, yr_sem), "z": (zs_sem, zr_sem)}[kind]
        made = Link(src, dst, ss.at[n], rs.at[n], device, sends, gets)
        links.append(made)
        return made

    def x_down(src, dst):
        return link("x", src, dst, (gx - 1, gy, gz), has_xm, has_xp)

    def x_up(src, dst):
        return link("x", src, dst, (gx + 1, gy, gz), has_xp, has_xm)

    def y_down(src, dst):
        return link("y", src, dst, (gx, gy - 1, gz), has_ym, has_yp)

    def y_up(src, dst):
        return link("y", src, dst, (gx, gy + 1, gz), has_yp, has_ym)

    def z_down(src, dst):
        return link("z", src, dst, (gx, gy, gz - 1), has_zm, has_zp)

    def z_up(src, dst):
        return link("z", src, dst, (gx, gy, gz + 1), has_zp, has_zm)

    def go(*those):
        for one in those:
            one.start()

    def got(*those):
        for one in those:
            one.arrive()

    for copy in loads[:2]:
        copy.wait()

    def weight(z):
        g = ld(md, z)
        for c in range(3):
            st(MA[c], z, g * ld(A1[c], z))

    every(weight)
    loads[2].wait()
    lo1 = V0 + MA
    pack_x(xa1, lo1, 0)
    pack_x(xb1, lo1 + [A1[0]], CX - 1)
    pack_y(ys1, lo1 + [A1[1]])

    pl.semaphore_wait(barrier, expected)

    zraw = [
        z_up(vel.at[:, CZ - 1], zl.at[0:3]),
        z_down(vel.at[:, 0], zu.at[0:3]),
        z_up(avel.at[:, CZ - 1], zl.at[3:6]),
        z_down(avel.at[:, 0], zu.at[3:6]),
        z_up(modulus.at[CZ - 1], zl.at[6]),
        z_down(modulus.at[0], zu.at[6]),
    ]
    r1x = [x_down(xa1, xh1), x_up(xb1, xl1)]
    r1y = [y_down(ys1, yh1), y_up(ys1, yl1)]
    go(*r1x, *r1y, *zraw)

    stage1 = []
    for step in range(1, NGY):
        other = lax.rem(gy + step, NGY)
        stage1.append(
            pltpu.make_async_remote_copy(
                src_ref=cs.at[pl.ds(pl.multiple_of(other * 32, 32), 32)],
                dst_ref=gath.at[mine],
                send_sem=f1s.at[step - 1], recv_sem=f1r.at[step - 1],
                device_id=(gx, other, gz), device_id_type=MESH,
            )
        )
        stage1[-1].start()

    loads[3].wait()
    loads[4].wait()
    got(*r1x, *r1y)

    @pl.when(has_xp)
    def _():
        unpack_x(xh1, lo1, CX)

    @pl.when(has_xm)
    def _():
        unpack_x(xl1, lo1 + [A1[0]], -1)

    every(lambda z: s1(z, yl1, yh1))
    pack_x(xa2, [p1, m1], 0)
    r2x = x_down(xa2, xh2)
    go(r2x)
    pack_y(ys2, [p1, m1])
    r2y = y_down(ys2, yh2)
    zpm = [
        z_down(p1.at[pl.ds(PITCH + 8, CX)], zu.at[13]),
        z_down(m1.at[pl.ds(PITCH + 8, CX)], zu.at[14]),
    ]
    go(r2y, *zpm)

    for copy in stage1:
        copy.wait_recv()
    rows = gath[...]
    r256 = lax.broadcasted_iota(jnp.int32, (256, CY), 0)
    l256 = lax.broadcasted_iota(jnp.int32, (256, CY), 1)
    codes = pltpu.roll(rows, 252, 0)
    hot = jnp.where(((r256 & 7) < 4) & (codes == (l256 + 1).astype(F32)), 1.0, 0.0)
    dense[...] = lax.dot_general(
        hot, rows, (((0,), (0,)), ((), ())), precision=HIGH, preferred_element_type=F32
    )
    stage2 = []
    for step in range(1, NGX):
        other = lax.rem(gx + step, NGX)
        stage2.append(
            pltpu.make_async_remote_copy(
                src_ref=dense.at[pl.ds(pl.multiple_of(other * 32, 32), 32)],
                dst_ref=hsum.at[step - 1],
                send_sem=f2s.at[step - 1], recv_sem=f2r.at[step - 1],
                device_id=(other, gy, gz), device_id_type=MESH,
            )
        )
        stage2[-1].start()

    got(r2x, r2y)

    @pl.when(has_xp)
    def _():
        unpack_x(xh2, [p1, m1], CX)

    every(lambda z: s2(z, yh2))

    lo3 = V1 + MA0
    pack_x(xa3, lo3, 0)
    pack_x(xb3, lo3 + [A0[0]], CX - 1)
    r3x = [x_down(xa3, xh3), x_up(xb3, xl3)]
    go(*r3x)
    pack_y(ys3, lo3 + [A0[1]])
    r3y = [y_down(ys3, yh3), y_up(ys3, yl3)]
    go(*r3y)
    first, final = pl.ds(PITCH + 8, CX), pl.ds(CZ * PITCH + 8, CX)
    zpart = [
        z_up(v1.at[:, final], zl.at[7:10]),
        z_down(v1.at[:, first], zu.at[7:10]),
        z_up(a0.at[:, final], zl.at[10:13]),
        z_down(a0.at[:, first], zu.at[10:13]),
    ]
    go(*zpart)

    for copy in stage2:
        copy.wait_recv()
    own = dense[pl.ds(pl.multiple_of(gx * 32, 32), 32), :]
    esum[...] = own + hsum[0] + hsum[1] + hsum[2]

    @pl.when(gz > 0)
    def _():
        to_surface = pltpu.make_async_remote_copy(
            src_ref=esum, dst_ref=ksum.at[gz - 1], send_sem=f3s, recv_sem=f3r.at[gz - 1],
            device_id=(gx, gy, 0), device_id_type=MESH,
        )
        to_surface.start()

    got(*r3x, *r3y)

    @pl.when(has_xp)
    def _():
        unpack_x(xh3, lo3, CX)

    @pl.when(has_xm)
    def _():
        unpack_x(xl3, lo3 + [A0[0]], -1)

    every(lambda z: s3(z, yl3, yh3))
    pack_x(xa4, [m0], 0)
    r4x = x_down(xa4, xh4)
    go(r4x)
    pack_y(ys4, [m0])
    r4y = y_down(ys4, yh4)
    go(r4y)
    got(r4x, r4y)

    @pl.when(has_xp)
    def _():
        unpack_x(xh4, [m0], CX)

    every(lambda z: s4(z, yh4))
    middle = pl.ds(3, CZ - 5)
    early = [
        pltpu.make_async_copy(out.at[:, middle], o_av.at[:, middle], out_sem.at[0]),
        pltpu.make_async_copy(
            m0.reshape(LAYERS, PITCH, CY).at[pl.ds(4, CZ - 5), pl.ds(8, CX), :], o_ap.at[middle], out_sem.at[1]
        ),
        pltpu.make_async_copy(sh.at[middle], o_sh.at[middle], out_sem.at[2]),
    ]
    for copy in early:
        copy.start()

    surface = gz == 0
    r5x = [
        link("x", xa5, xh5, (gx - 1, gy, gz), surface & has_xm, surface & has_xp),
        link("x", xb5, xl5, (gx + 1, gy, gz), surface & has_xp, surface & has_xm),
    ]
    r5y = [
        link("y", ys5, yh5, (gx, gy - 1, gz), surface & has_ym, surface & has_yp),
        link("y", ys5, yl5, (gx, gy + 1, gz), surface & has_yp, surface & has_ym),
    ]

    @pl.when(surface)
    def _():
        for other in range(1, NGZ):
            pltpu.make_async_remote_copy(
                src_ref=esum, dst_ref=ksum.at[other - 1], send_sem=f3s, recv_sem=f3r.at[other - 1],
                device_id=(gx, gy, 1), device_id_type=MESH,
            ).wait_recv()
        total = esum[...]
        for other in range(1, NGZ):
            total = total + ksum[other - 1]
        esum[...] = total
        w = ld(A1[2], 0) + total[CX:2 * CX]
        st(A1[2], 0, w)
        w = w * ld(md, 0)
        st(MA[2], 0, w)
        pack_rows(xa5, [(MA[2], 0)], 0)
        pack_rows(xb5, [(MA[2], 0)], CX - 1)
        ys5[...] = pltpu.roll(w, 11, 1)

    go(*r5x, *r5y)
    got(*r5x, *r5y)

    @pl.when(surface & has_xp)
    def _():
        unpack_rows(xh5, [(MA[2], 0)], CX)

    @pl.when(surface & has_xm)
    def _():
        unpack_rows(xl5, [(MA[2], 0)], -1)

    @pl.when(surface & has_yp)
    def _():
        yh1[0] = jnp.where(lane == 11, yh5[...], yh1[0])

    @pl.when(surface & has_ym)
    def _():
        yl1[0] = jnp.where(lane == 10, yl5[...], yl1[0])

    for one in zpart + zpm:
        one.flush()
    got(*zraw, *zpm, *zpart)

    @pl.when(has_zm)
    def _():
        for c in range(3):
            st(V0[c], -1, zl[c])
            st(MA[c], -1, zl[6] * zl[3 + c])
        st(A1[2], -1, zl[5])

    @pl.when(has_zp)
    def _():
        for c in range(3):
            st(V0[c], CZ, zu[c])
            st(MA[c], CZ, zu[6] * zu[3 + c])
        st(p1, CZ, zu[13] - ld(V0[2], CZ - 1))
        st(m1, CZ, zu[14] + 0.25 * ld(A1[2], CZ - 1))

    def some(fn, layers):
        for z in layers:
            fn(z)

    some(lambda z: s1(z, yl1, yh1), (0, 1, CZ - 1))
    x6 = [(p1, 0), (m1, 0), (m1, 1), (A1[2], CZ - 1)]
    pack_rows(xa6, x6, 0)
    r6x = x_down(xa6, xh6)
    go(r6x)
    pack_y(ys6, [p1, m1, A1[2]])
    r6y = y_down(ys6, yh6)
    go(r6y)
    got(r6x, r6y)

    @pl.when(has_xp)
    def _():
        unpack_rows(xh6, x6, CX)

    some(lambda z: s2(z, yh6), (0, 1, CZ - 1))

    @pl.when(surface)
    def _():
        w = ld(A0[2], 0) + esum[0:CX, :]
        st(A0[2], 0, w)
        st(MA0[2], 0, w * ld(md, 0))

    @pl.when(has_zm)
    def _():
        g = zl[6]
        extra_v, extra_a = ld(p1, 0), ld(m1, 0)
        for c in range(3):
            v = g * ld(V0[c], 0)
            a = 0.25 * ld(MA[c], 0)
            if c == 2:
                v, a = v + extra_v, a - extra_a
            st(V1[c], -1, zl[7 + c] + 0.25 * v)
            a = zl[10 + c] + a
            st(A0[c], -1, a)
            st(MA0[c], -1, g * a)

    @pl.when(has_zp)
    def _():
        g = zu[6]
        top = CZ - 1
        q, w = ld(V0[2], top), ld(A1[2], top)
        gq = (ld(V0[2], top, 1) - q, yhi(q, yh1, top, 2) - q, -q)
        gw = (ld(A1[2], top, 1) - w, yhi(w, yh6, top, 2) - w, -w)
        for c in range(3):
            st(V1[c], CZ, zu[7 + c] + 0.25 * (g * ld(V0[c], top) - gq[c]))
            a = zu[10 + c] + 0.25 * (ld(MA[c], top) - gw[c])
            st(A0[c], CZ, a)
            st(MA0[c], CZ, g * a)

    x7 = [(ref, z) for ref in lo3 for z in (0, 1, CZ - 1)]
    x7up = x7 + [(A0[0], z) for z in (0, 1, CZ - 1, CZ)]
    pack_rows(xa7, x7, 0)
    pack_rows(xb7, x7up, CX - 1)
    r7x = [x_down(xa7, xh7), x_up(xb7, xl7)]
    go(*r7x)
    pack_y(ys7, lo3 + [A0[1]], last=A0[1])
    r7y = [y_down(ys7, yh7), y_up(ys7, yl7)]
    go(*r7y)
    got(*r7x, *r7y)

    @pl.when(has_xp)
    def _():
        unpack_rows(xh7, x7, CX)

    @pl.when(has_xm)
    def _():
        unpack_rows(xl7, x7up, -1)

    edges = (0, 1, 2, CZ - 2, CZ - 1)
    some(lambda z: s3(z, yl7, yh7), edges)

    @pl.when(has_zp)
    def _():
        x, y, w = (ld(r, CZ) for r in A0)
        low = jnp.where(lane == 0, pltpu.roll(yl7[3], 2, 1), pltpu.roll(y, 1, 1))
        d = (x - ld(A0[0], CZ, -1)) + (y - low) + (w - ld(A0[2], CZ - 1))
        st(m0, CZ, ld(m1, CZ) - 0.25 * d)

    x8 = [(m0, z) for z in (0, 1, 2, CZ - 1)]
    pack_rows(xa8, x8, 0)
    r8x = x_down(xa8, xh8)
    go(r8x)
    pack_y(ys8, [m0])
    r8y = y_down(ys8, yh8)
    go(r8y)
    got(r8x, r8y)

    @pl.when(has_xp)
    def _():
        unpack_rows(xh8, x8, CX)

    some(lambda z: s4(z, yh8), edges)
    late = []
    for n, (start, size) in enumerate(((0, 3), (CZ - 2, 2))):
        part = pl.ds(start, size)
        late += [
            pltpu.make_async_copy(out.at[:, part], o_av.at[:, part], out_sem.at[3 + 3 * n]),
            pltpu.make_async_copy(
                m0.reshape(LAYERS, PITCH, CY).at[pl.ds(start + 1, size), pl.ds(8, CX), :],
                o_ap.at[part], out_sem.at[4 + 3 * n],
            ),
            pltpu.make_async_copy(sh.at[part], o_sh.at[part], out_sem.at[5 + 3 * n]),
        ]
    for copy in late:
        copy.start()
    for one in links:
        if one not in zpart and one not in zpm:
            one.flush()
    for copy in stage1 + stage2:
        copy.wait_send()

    @pl.when(gz > 0)
    def _():
        pltpu.make_async_remote_copy(
            src_ref=esum, dst_ref=ksum.at[gz - 1], send_sem=f3s, recv_sem=f3r.at[gz - 1],
            device_id=(gx, gy, 0), device_id_type=MESH,
        ).wait_send()

    for copy in early + late:
        copy.wait()


def shards(vel, pres, modulus, avel, apres, svals, sowner, sline, sstep):
    vector = pltpu.VMEM((3, ROWS, CY), F32)
    scalar = pltpu.VMEM((ROWS, CY), F32)
    flat3 = pltpu.VMEM((3, CZ, CX, CY), F32)
    flat = pltpu.VMEM((CZ, CX, CY), F32)
    pack = pltpu.VMEM((4, CX, CY), F32)
    plane = pltpu.VMEM((CX, CY), F32)

    def lines(n):
        return pltpu.VMEM((n, CY), F32)

    def dma(n):
        return pltpu.SemaphoreType.DMA((n,))

    anywhere, inside = pl.BlockSpec(memory_space=pl.ANY), pl.BlockSpec(memory_space=pltpu.VMEM)
    return pl.pallas_call(
        body,
        out_shape=(
            jax.ShapeDtypeStruct((3, CZ, CX, CY), F32),
            jax.ShapeDtypeStruct((CZ, CX, CY), F32),
            jax.ShapeDtypeStruct((CZ, CX, CY), F32),
        ),
        in_specs=[anywhere] * 5 + [inside] * 4,
        out_specs=(anywhere,) * 3,
        scratch_shapes=[
            vector, vector, vector, scalar, scalar, scalar, vector, vector, vector, scalar,
            flat, flat, flat3, flat3, flat3, flat, flat3,
            pack, pack, pack, pack, pack, pack, pack, pack, pack, pack,
            plane, plane, plane, pack, pack, pack, pack, pack, pack, pack,
            lines(6 * CZ), lines(7 * CZ), lines(6 * CZ), lines(7 * CZ),
            lines(2 * CZ), lines(2 * CZ),
            lines(6 * CZ), lines(7 * CZ), lines(6 * CZ), lines(7 * CZ),
            lines(CZ), lines(CZ),
            lines(8), lines(8), lines(8), lines(8), lines(8), lines(8),
            lines(24), lines(24), lines(24), lines(24), lines(8), lines(8),
            pltpu.VMEM((13, CX, CY), F32), pltpu.VMEM((15, CX, CY), F32),
            lines(256), lines(256), lines(CY), pltpu.VMEM((3, 32, CY), F32), lines(32),
            pltpu.VMEM((NGZ - 1, 32, CY), F32),
            dma(5), dma(9), dma(12), dma(12), dma(12), dma(12), dma(12), dma(12),
            dma(NGY - 1), dma(NGY - 1), dma(NGX - 1), dma(NGX - 1),
            pltpu.SemaphoreType.DMA, dma(NGZ - 1),
        ],
        compiler_params=pltpu.CompilerParams(
            collective_id=0, has_side_effects=True, vmem_limit_bytes=48 * 2**20
        ),
        cost_estimate=pl.CostEstimate(flops=20_000_000, bytes_accessed=3_670_016, transcendentals=0),
        name="adjoint",
    )(vel, pres, modulus, avel, apres, svals, sowner, sline.reshape(1, 32), sstep.reshape(1, 32))


def solution(mesh):
    return jax.shard_map(
        shards,
        mesh=mesh,
        in_specs=(
            P(None, "gz", "gx", "gy"),
            P("gz", "gx", "gy"),
            P("gz", "gx", "gy"),
            P(None, "gz", "gx", "gy"),
            P("gz", "gx", "gy"),
            P(("gx", "gy", "gz"), None),
            P(("gx", "gy", "gz"), None),
            P(("gx", "gy", "gz")),
            P(("gx", "gy", "gz")),
        ),
        out_specs=(P(None, "gz", "gx", "gy"), P("gz", "gx", "gy"), P("gz", "gx", "gy")),
        check_vma=False,
    )
```

time: 411 us -> 62.8 us (0.15)
  the two profiles are of different devices: /device:TPU:113 before, /device:TPU:25 now
where the time goes in v1:
time: 62.8 us; the launch traced here: 62.4 us
  Pallas kernels  53.6 us (85%)
  local copies, waits for them, and re-layouts  8.16 us (13%)
  between operations  0.69 us (1%)
    pallas_call x1, Pallas kernels, shards(): pl.pallas_call(body, out_shape=(jax.ShapeDtypeStruct((3, CZ, CX, CY), F32...  53.6 us
    unnamed x20, local copies, waits for them, and re-layouts  8.16 us

profile of v1, /device:TPU:25, one launch (start us, length us, event | category | flops | bytes accessed | tf_op | source)
XLA Modules:
  0.0 62.4 jit_solution(14922343219838253050)
XLA Ops:
  0.6 0.0 copy-start.5
  0.6 0.0 copy-start.6
  0.7 0.0 copy-start.7
  0.7 0.8 %copy.12.sowner = s32[32,1]{1,0:T(8,128)S(1)} copy(s32[32,1]{0,1:T(1,128)} %param.15) | data formatting | bytes 256 | tf_op args[6]
  1.4 0.0 copy-done.5
  1.4 0.0 copy-done.6
  1.4 0.0 copy-done.7
  1.4 0.0 copy-start
  1.4 1.1 %copy-done = f32[3,32,16,128]{3,2,1,0:T(8,128)S(1)} copy-done((f32[3,32,16,128]{3,2,1,0:T(8,128)S(1)}, f32[3,32,16,128]{3,2,1,0:T(8,128)}, u32[]{:S(2)}) %copy-start) | copy-done | bytes 786456
  2.6 0.0 copy-start.1
  2.6 1.1 %copy-done.1 = f32[3,32,16,128]{3,2,1,0:T(8,128)S(1)} copy-done((f32[3,32,16,128]{3,2,1,0:T(8,128)S(1)}, f32[3,32,16,128]{3,2,1,0:T(8,128)}, u32[]{:S(2)}) %copy-start.1) | copy-done | bytes 786456
  3.7 0.0 copy-start.2
  3.7 0.9 %copy-done.2 = f32[32,16,128]{2,1,0:T(8,128)S(1)} copy-done((f32[32,16,128]{2,1,0:T(8,128)S(1)}, f32[32,16,128]{2,1,0:T(8,128)}, u32[]{:S(2)}) %copy-start.2) | copy-done | bytes 262168
  4.7 0.0 copy-start.3
  4.7 0.9 %copy-done.3 = f32[32,16,128]{2,1,0:T(8,128)S(1)} copy-done((f32[32,16,128]{2,1,0:T(8,128)S(1)}, f32[32,16,128]{2,1,0:T(8,128)}, u32[]{:S(2)}) %copy-start.3) | copy-done | bytes 262168
  5.6 0.0 copy-start.4
  5.6 0.9 %copy-done.4 = f32[32,16,128]{2,1,0:T(8,128)S(1)} copy-done((f32[32,16,128]{2,1,0:T(8,128)S(1)}, f32[32,16,128]{2,1,0:T(8,128)}, u32[]{:S(2)}) %copy-start.4) | copy-done | bytes 262168
  6.6 53.6 %adjoint.1 = (f32[3,32,16,128]{3,2,1,0:T(8,128)S(1)}, f32[32,16,128]{2,1,0:T(8,128)S(1)}, f32[32,16,128]{2,1,0:T(8,128)S(1)}) custom-call(f32[3,32,16,128]{3,2,1,0:T(8,128)S(1)} %copy-done, f32[32,16,128]{2,1,0:T(8,128)S(1)} %copy-done.2, f32[32,16,128]{2,1,0:T(8,128)S(1)} %copy-done.3, f32[3,32,16,128]{3,2,1,0:T(8,128)S(1)} %copy-done.1, ...), custom_call_target="tpu_custom_call" | custom-call | flops 20000000 | bytes 3670016 | tf_op jit(solution)/shard_map/adjoint/pallas_call | solution.py:655
  60.2 0.9 %copy.16 = f32[3,32,16,128]{3,2,1,0:T(8,128)} copy(f32[3,32,16,128]{3,2,1,0:T(8,128)S(1)} %get-tuple-element.6) | data formatting | bytes 1572864
  61.0 0.7 %copy.17 = f32[32,16,128]{2,1,0:T(8,128)} copy(f32[32,16,128]{2,1,0:T(8,128)S(1)} %get-tuple-element.7) | data formatting | bytes 524288
  61.7 0.7 %copy.18 = f32[32,16,128]{2,1,0:T(8,128)} copy(f32[32,16,128]{2,1,0:T(8,128)S(1)} %get-tuple-element.8) | data formatting | bytes 524288
Async XLA Ops:
  0.6 0.8 %copy-start.5 = (f32[32,128]{1,0:T(8,128)S(1)}, f32[32,128]{1,0:T(8,128)}, u32[]{:S(2)}) copy-start(f32[32,128]{1,0:T(8,128)} %svals.1) | copy-start | bytes 49156
  0.6 0.8 %copy-start.6 = (s32[32]{0:T(128)S(1)}, s32[32]{0:T(128)}, u32[]{:S(2)}) copy-start(s32[32]{0:T(128)} %param.16) | copy-start | bytes 388
  0.7 0.8 %copy-start.7 = (s32[32]{0:T(128)S(1)}, s32[32]{0:T(128)}, u32[]{:S(2)}) copy-start(s32[32]{0:T(128)} %param.17) | copy-start | bytes 388
  1.4 1.1 %copy-start = (f32[3,32,16,128]{3,2,1,0:T(8,128)S(1)}, f32[3,32,16,128]{3,2,1,0:T(8,128)}, u32[]{:S(2)}) copy-start(f32[3,32,16,128]{3,2,1,0:T(8,128)} %vel.1) | copy-start | bytes 2359300
  2.6 1.1 %copy-start.1 = (f32[3,32,16,128]{3,2,1,0:T(8,128)S(1)}, f32[3,32,16,128]{3,2,1,0:T(8,128)}, u32[]{:S(2)}) copy-start(f32[3,32,16,128]{3,2,1,0:T(8,128)} %avel.1) | copy-start | bytes 2359300
  3.7 0.9 %copy-start.2 = (f32[32,16,128]{2,1,0:T(8,128)S(1)}, f32[32,16,128]{2,1,0:T(8,128)}, u32[]{:S(2)}) copy-start(f32[32,16,128]{2,1,0:T(8,128)} %pres.1) | copy-start | bytes 786436
  4.7 0.9 %copy-start.3 = (f32[32,16,128]{2,1,0:T(8,128)S(1)}, f32[32,16,128]{2,1,0:T(8,128)}, u32[]{:S(2)}) copy-start(f32[32,16,128]{2,1,0:T(8,128)} %modulus.1) | copy-start | bytes 786436
  5.6 0.9 %copy-start.4 = (f32[32,16,128]{2,1,0:T(8,128)S(1)}, f32[32,16,128]{2,1,0:T(8,128)}, u32[]{:S(2)}) copy-start(f32[32,16,128]{2,1,0:T(8,128)} %apres.1) | copy-start | bytes 786436

commit v2 on v1

v2 whole, which is shorter than its diff:
```python
import jax
import jax.numpy as jnp
from jax import lax
from jax.experimental import pallas as pl
from jax.experimental.pallas import tpu as pltpu
from jax.sharding import PartitionSpec as P

MESH = pl.DeviceIdType.MESH
F32 = jnp.float32
CZ, CX, CY = 32, 16, 128
PITCH = 32
LAYERS = CZ + 2
ROWS = LAYERS * PITCH
NGX, NGY, NGZ = 4, 8, 8
UNROLL = 4
HIGH = lax.Precision.HIGHEST


def body(
    vel, pres, modulus, avel, apres, svals_h, sowner_h, sline_h, sstep_h,
    o_av, o_ap, o_sh,
    v0, a1, ma, md, p1, m1, v1, a0, ma0, m0,
    p0, ap, bend0, lm, lm0, sh, out,
    ys1, yl1, yh1, ys2, yh2, ys3, yl3, yh3, ys4, yh4,
    c1, c3, c7, ys9, yh9, xa9, xb9, xl9, xh9, xa10, xh10,
    ys5, yl5, yh5, ys6, yh6, ys7, yl7, yh7, ys8, yh8,
    xa1, xb1, xh1, xl1, xa2, xh2, xa3, xb3, xh3, xl3, xa4, xh4,
    xa5, xb5, xh5, xl5, xa6, xh6, xa7, xb7, xh7, xl7, xa8, xh8,
    svals, sowner, sline, sstep,
    zl, zu, cs, gath, dense, hsum, esum, ksum,
    in_sem, out_sem, xs_sem, xr_sem, ys_sem, yr_sem, zs_sem, zr_sem,
    f1s, f1r, f2s, f2r, f3s, f3r,
):
    gx, gy, gz = lax.axis_index("gx"), lax.axis_index("gy"), lax.axis_index("gz")
    has_xm, has_xp = gx > 0, gx < NGX - 1
    has_ym, has_yp = gy > 0, gy < NGY - 1
    has_zm, has_zp = gz > 0, gz < NGZ - 1
    barrier = pltpu.get_barrier_semaphore()

    def grid3(ref):
        if len(ref.shape) == 3:
            return ref.reshape(3, LAYERS, PITCH, CY).at[:, pl.ds(1, CZ), pl.ds(8, CX), :]
        return ref.reshape(LAYERS, PITCH, CY).at[pl.ds(1, CZ), pl.ds(8, CX), :]

    loads = [
        pltpu.make_async_copy(src, dst, in_sem.at[i])
        for i, (src, dst) in enumerate(
            [(avel, grid3(a1)), (modulus, grid3(md)), (vel, grid3(v0)), (pres, p0), (apres, ap)]
        )
    ]
    sensors = [
        pltpu.make_async_copy(src, dst, in_sem.at[5 + i])
        for i, (src, dst) in enumerate(
            [(svals_h, svals), (sowner_h, sowner), (sline_h, sline), (sstep_h, sstep)]
        )
    ]
    for copy in loads + sensors:
        copy.start()

    lane = lax.broadcasted_iota(jnp.int32, (CX, CY), 1)

    @pl.when(jnp.logical_not(has_ym))
    def _():
        for ref in (yl1, yl3, yl7):
            ref[...] = jnp.zeros(ref.shape, F32)
        yl5[...] = jnp.zeros(yl5.shape, F32)

    @pl.when(jnp.logical_not(has_yp))
    def _():
        for ref in (yh1, yh2, yh3, yh4, yh6, yh7, yh8, yh9):
            ref[...] = jnp.zeros(ref.shape, F32)
        yh5[...] = jnp.zeros(yh5.shape, F32)

    def greet(device):
        pl.semaphore_signal(barrier, inc=1, device_id=device, device_id_type=MESH)

    @pl.when(has_zm)
    def _():
        greet((gx, gy, gz - 1))

    @pl.when(has_zp)
    def _():
        greet((gx, gy, gz + 1))

    @pl.when(gz == 0)
    def _():
        for other in range(2, NGZ):
            greet((gx, gy, other))

    for step in range(1, NGY):
        greet((gx, lax.rem(gy + step, NGY), gz))
    for step in range(1, NGX):
        greet((lax.rem(gx + step, NGX), gy, gz))
    expected = (
        NGX - 1 + NGY - 1
        + has_zm.astype(jnp.int32) + has_zp.astype(jnp.int32) + (gz >= 2).astype(jnp.int32)
    )

    def comps(ref):
        return [ref.at[c] for c in range(3)]

    V0, A1, MA, V1, A0, MA0 = (comps(r) for r in (v0, a1, ma, v1, a0, ma0))

    zeros_layer = jnp.zeros((PITCH, CY), F32)
    zeros_rows = jnp.zeros((LAYERS, CY), F32)
    for ref in V0 + A1 + MA + V1 + A0 + MA0 + [p1, m1, m0]:
        ref[0:PITCH, :] = zeros_layer
        ref[ROWS - PITCH:ROWS, :] = zeros_layer

    @pl.when(jnp.logical_not(has_xm))
    def _():
        for ref in V0 + [A1[0]] + MA + V1 + [A0[0]] + MA0:
            ref[pl.ds(7, LAYERS, stride=PITCH), :] = zeros_rows

    @pl.when(jnp.logical_not(has_xp))
    def _():
        for ref in V0 + MA + [A1[2]] + V1 + MA0 + [p1, m1, m0]:
            ref[pl.ds(24, LAYERS, stride=PITCH), :] = zeros_rows

    def ld(ref, z, dx=0):
        return ref[pl.ds((z + 1) * PITCH + 8 + dx, CX), :]

    def st(ref, z, value):
        ref[pl.ds(pl.multiple_of((z + 1) * PITCH + 8, 8), CX), :] = value

    def halo(blk, z, f):
        return pltpu.roll(blk[z & 3], (CY - ((z >> 2) * 16 + 2 * f)) & (CY - 1), 1)

    def ylo(u, blk, z, f):
        return jnp.where(lane == 0, halo(blk, z, f), pltpu.roll(u, 1, 1))

    def yhi(u, blk, z, f):
        shift = CY - 2 - (z >> 2) * 16 - 2 * f
        return jnp.where(lane == CY - 1, pltpu.roll(blk[z & 3], shift, 1), pltpu.roll(u, CY - 1, 1))

    def merge(dst, low, high, planes=range(4)):
        for zz in planes:
            dst[zz] = jnp.where((lane & 1) == 0, low[zz], pltpu.roll(high[zz], CY - 2, 1))

    def lap(ref, z, blk, f):
        c = ld(ref, z)
        h = halo(blk, z, f)
        low = jnp.where(lane == 0, h, pltpu.roll(c, 1, 1))
        high = jnp.where(lane == CY - 1, h, pltpu.roll(c, CY - 1, 1))
        total = ld(ref, z, 1) + ld(ref, z, -1) + (ld(ref, z + 1) + ld(ref, z - 1))
        return total + (low + high) - 6.0 * c, low

    def div(refs, z, low):
        x, y, w = (ld(r, z) for r in refs)
        return (x - ld(refs[0], z, -1)) + (y - low) + (w - ld(refs[2], z - 1))

    def grad(ref, z, yh, f):
        q = ld(ref, z)
        return ld(ref, z, 1) - q, yhi(q, yh, z, f) - q, ld(ref, z + 1) - q

    def s1(z, blk):
        lows = []
        for c in range(3):
            bend0[c, z], low = lap(V0[c], z, blk, c)
            lows.append(low)
            lm[c, z], _ = lap(MA[c], z, blk, 3 + c)
        st(p1, z, p0[z] + div(V0, z, lows[1]))
        st(m1, z, ap[z] - 0.25 * div(A1, z, ylo(ld(A1[1], z), blk, z, 6)))

    def s2(z, yh):
        gp, gm = grad(p1, z, yh, 0), grad(m1, z, yh, 1)
        g = ld(md, z)
        for c in range(3):
            st(V1[c], z, ld(V0[c], z) + 0.25 * (gp[c] + g * bend0[c, z]))
            new = ld(A1[c], z) + 0.25 * lm[c, z] - gm[c]
            st(A0[c], z, new)
            st(MA0[c], z, g * new)

    def s3(z, blk):
        total = None
        for c in range(3):
            part = ld(A1[c], z) * lap(V1[c], z, blk, c)[0] + ld(A0[c], z) * bend0[c, z]
            total = part if total is None else total + part
            lm0[c, z], _ = lap(MA0[c], z, blk, 3 + c)
        sh[z] = 0.25 * total
        st(m0, z, ld(m1, z) - 0.25 * div(A0, z, ylo(ld(A0[1], z), blk, z, 6)))

    def s4(z, yh):
        gm = grad(m0, z, yh, 0)
        for c in range(3):
            out[c, z] = ld(A0[c], z) + 0.25 * lm0[c, z] - gm[c]

    def every(fn, start=0, stop=CZ, unroll=UNROLL):
        turns = (stop - start) // unroll

        def step(n, carry):
            for k in range(unroll):
                fn(start + n * unroll + k)
            return carry

        lax.fori_loop(0, turns, step, 0)
        for z in range(start + turns * unroll, stop):
            fn(z)

    def some(fn, layers):
        for z in layers:
            fn(z)

    def pack_y(dst, fields):
        def step(zz, carry):
            acc = jnp.zeros((CX, CY), F32)
            for g in range(8):
                for f, ref in enumerate(fields):
                    s = g * 16 + 2 * f + 1
                    acc = jnp.where((lane >> 1) == (s >> 1), pltpu.roll(ld(ref, g * 4 + zz), s, 1), acc)
            dst[zz] = acc
            return carry
        lax.fori_loop(0, 4, step, 0)

    def pack_layers(dst, fields, layers, last=None):
        for zz in range(4):
            acc = jnp.zeros((CX, CY), F32)
            for z in layers:
                if z % 4 == zz:
                    for f, ref in enumerate(fields):
                        s = (z // 4) * 16 + 2 * f + 1
                        acc = jnp.where((lane >> 1) == (s >> 1), pltpu.roll(ld(ref, z), s, 1), acc)
            if zz == 3 and last is not None:
                acc = jnp.where(lane >= CY - 2, pltpu.roll(ld(last, CZ), CY - 1, 1), acc)
            dst[zz] = acc

    def face(ref, x):
        return ref[pl.ds(PITCH + 8 + x, CZ, stride=PITCH), :]

    def pack_x(dst, fields, x):
        for i, ref in enumerate(fields):
            dst[i * CZ:(i + 1) * CZ, :] = face(ref, x)

    def unpack_x(src, fields, x):
        for i, ref in enumerate(fields):
            ref[pl.ds(PITCH + 8 + x, CZ, stride=PITCH), :] = src[i * CZ:(i + 1) * CZ, :]

    def rows_of(pairs, x):
        return [(ref, (z + 1) * PITCH + 8 + x) for ref, z in pairs]

    def pack_rows(dst, pairs, x):
        for i, (ref, row) in enumerate(rows_of(pairs, x)):
            dst[i:i + 1, :] = ref[row:row + 1, :]

    def unpack_rows(src, pairs, x):
        for i, (ref, row) in enumerate(rows_of(pairs, x)):
            ref[row:row + 1, :] = src[i:i + 1, :]

    def store(start, size, n):
        part = pl.ds(start, size)
        copies = [
            pltpu.make_async_copy(out.at[:, part], o_av.at[:, part], out_sem.at[3 * n]),
            pltpu.make_async_copy(
                m0.reshape(LAYERS, PITCH, CY).at[pl.ds(start + 1, size), pl.ds(8, CX), :],
                o_ap.at[part], out_sem.at[3 * n + 1],
            ),
            pltpu.make_async_copy(sh.at[part], o_sh.at[part], out_sem.at[3 * n + 2]),
        ]
        for copy in copies:
            copy.start()
        return copies

    class Link:
        def __init__(self, src, dst, send, recv, device, sends, gets):
            self.copy = pltpu.make_async_remote_copy(
                src_ref=src, dst_ref=dst, send_sem=send, recv_sem=recv,
                device_id=device, device_id_type=MESH,
            )
            self.sends, self.gets = sends, gets

        def start(self):
            pl.when(self.sends)(self.copy.start)

        def arrive(self):
            pl.when(self.gets)(self.copy.wait_recv)

        def flush(self):
            pl.when(self.sends)(self.copy.wait_send)

    links = []
    counts = {"x": 0, "y": 0, "z": 0}

    def link(kind, src, dst, device, sends, gets):
        n = counts[kind]
        counts[kind] += 1
        ss, rs = {"x": (xs_sem, xr_sem), "y": (ys_sem, yr_sem), "z": (zs_sem, zr_sem)}[kind]
        made = Link(src, dst, ss.at[n], rs.at[n], device, sends, gets)
        links.append(made)
        return made

    def x_down(src, dst):
        return link("x", src, dst, (gx - 1, gy, gz), has_xm, has_xp)

    def x_up(src, dst):
        return link("x", src, dst, (gx + 1, gy, gz), has_xp, has_xm)

    def y_down(src, dst):
        return link("y", src, dst, (gx, gy - 1, gz), has_ym, has_yp)

    def y_up(src, dst):
        return link("y", src, dst, (gx, gy + 1, gz), has_yp, has_ym)

    def z_down(src, dst):
        return link("z", src, dst, (gx, gy, gz - 1), has_zm, has_zp)

    def z_up(src, dst):
        return link("z", src, dst, (gx, gy, gz + 1), has_zp, has_zm)

    def go(*those):
        for one in those:
            one.start()

    def got(*those):
        for one in those:
            one.arrive()

    for copy in loads:
        copy.wait()

    def weight(z):
        g = ld(md, z)
        for c in range(3):
            st(MA[c], z, g * ld(A1[c], z))

    every(weight)
    lo1 = V0 + MA
    rim = (0, 1, CZ - 1)
    x9 = [(ref, z) for ref in lo1 for z in rim]
    x9up = x9 + [(A1[0], z) for z in rim]
    pack_rows(xa9, x9, 0)
    pack_rows(xb9, x9up, CX - 1)
    pack_y(ys1, lo1 + [A1[1]])

    pl.semaphore_wait(barrier, expected)

    r9x = [x_down(xa9, xh9), x_up(xb9, xl9)]
    r1y = [y_down(ys1, yh1), y_up(ys1, yl1)]
    r1x = [x_down(xa1, xh1), x_up(xb1, xl1)]
    zraw = [
        z_up(vel.at[:, CZ - 1], zl.at[0:3]),
        z_down(vel.at[:, 0], zu.at[0:3]),
        z_up(avel.at[:, CZ - 1], zl.at[3:6]),
        z_down(avel.at[:, 0], zu.at[3:6]),
        z_up(modulus.at[CZ - 1], zl.at[6]),
        z_down(modulus.at[0], zu.at[6]),
    ]
    go(*r9x, *r1y, *zraw)
    pack_x(xa1, lo1, 0)
    pack_x(xb1, lo1 + [A1[0]], CX - 1)
    go(*r1x)

    for copy in sensors:
        copy.wait()
    owner_row = sowner[...].astype(F32)
    r0 = lax.broadcasted_iota(jnp.int32, (32, 32), 0)
    r1 = lax.broadcasted_iota(jnp.int32, (32, 32), 1)
    owner_col = jnp.sum(jnp.where(r0 == r1, owner_row, 0.0), axis=1, keepdims=True)
    rank = jnp.sum(
        jnp.where((owner_col == owner_row) & (r0 < r1), 1.0, 0.0), axis=0, keepdims=True
    ).astype(jnp.int32)
    owner_int = owner_row.astype(jnp.int32)
    own_gx, own_gy = owner_int >> 3, owner_int & 7
    place = own_gy * 32 + own_gx * 8 + rank
    code_row = (own_gx * 32 + sstep[...] * CX + sline[...] + 1).astype(F32)
    code_col = jnp.sum(jnp.where(r0 == r1, code_row, 0.0), axis=1, keepdims=True)
    slot = lax.broadcasted_iota(jnp.int32, (256, 32), 0)
    cs[...] = jnp.dot(
        (slot == place).astype(F32), svals[...], precision=HIGH, preferred_element_type=F32
    ) + jnp.dot(
        (slot == place + 4).astype(F32), jnp.broadcast_to(code_col, (32, CY)),
        precision=HIGH, preferred_element_type=F32,
    )
    mine = pl.ds(pl.multiple_of(gy * 32, 32), 32)
    gath[mine, :] = cs[mine, :]

    stage1 = []
    for step in range(1, NGY):
        other = lax.rem(gy + step, NGY)
        stage1.append(
            pltpu.make_async_remote_copy(
                src_ref=cs.at[pl.ds(pl.multiple_of(other * 32, 32), 32)],
                dst_ref=gath.at[mine],
                send_sem=f1s.at[step - 1], recv_sem=f1r.at[step - 1],
                device_id=(gx, other, gz), device_id_type=MESH,
            )
        )
        stage1[-1].start()

    got(*r9x, *r1y)

    @pl.when(has_xp)
    def _():
        unpack_rows(xh9, x9, CX)

    @pl.when(has_xm)
    def _():
        unpack_rows(xl9, x9up, -1)

    merge(c1, yl1, yh1)
    some(lambda z: s1(z, c1), rim)
    x10 = [(ref, z) for ref in (p1, m1) for z in (0, CZ - 1)]
    pack_rows(xa10, x10, 0)
    r10x = x_down(xa10, xh10)
    go(r10x)
    pack_layers(ys9, [p1, m1], (0, CZ - 1))
    r9y = y_down(ys9, yh9)
    zpm = [
        z_down(p1.at[pl.ds(PITCH + 8, CX)], zu.at[13]),
        z_down(m1.at[pl.ds(PITCH + 8, CX)], zu.at[14]),
    ]
    go(r9y, *zpm)
    got(r10x, r9y)

    @pl.when(has_xp)
    def _():
        unpack_rows(xh10, x10, CX)

    some(lambda z: s2(z, yh9), (0, CZ - 1))
    first, final = pl.ds(PITCH + 8, CX), pl.ds(CZ * PITCH + 8, CX)
    zpart = [
        z_up(v1.at[:, final], zl.at[7:10]),
        z_down(v1.at[:, first], zu.at[7:10]),
        z_up(a0.at[:, final], zl.at[10:13]),
        z_down(a0.at[:, first], zu.at[10:13]),
    ]
    go(*zpart)

    for copy in stage1:
        copy.wait_recv()
    rows = gath[...]
    r256 = lax.broadcasted_iota(jnp.int32, (256, CY), 0)
    l256 = lax.broadcasted_iota(jnp.int32, (256, CY), 1)
    codes = pltpu.roll(rows, 252, 0)
    hot = jnp.where(((r256 & 7) < 4) & (codes == (l256 + 1).astype(F32)), 1.0, 0.0)
    dense[...] = lax.dot_general(
        hot, rows, (((0,), (0,)), ((), ())), precision=HIGH, preferred_element_type=F32
    )
    stage2 = []
    for step in range(1, NGX):
        other = lax.rem(gx + step, NGX)
        stage2.append(
            pltpu.make_async_remote_copy(
                src_ref=dense.at[pl.ds(pl.multiple_of(other * 32, 32), 32)],
                dst_ref=hsum.at[step - 1],
                send_sem=f2s.at[step - 1], recv_sem=f2r.at[step - 1],
                device_id=(other, gy, gz), device_id_type=MESH,
            )
        )
        stage2[-1].start()

    got(*r1x)

    @pl.when(has_xp)
    def _():
        unpack_x(xh1, lo1, CX)

    @pl.when(has_xm)
    def _():
        unpack_x(xl1, lo1 + [A1[0]], -1)

    every(lambda z: s1(z, c1), 2, CZ - 1)
    pack_x(xa2, [p1, m1], 0)
    r2x = x_down(xa2, xh2)
    go(r2x)
    pack_y(ys2, [p1, m1])
    r2y = y_down(ys2, yh2)
    go(r2y)

    for copy in stage2:
        copy.wait_recv()
    own = dense[pl.ds(pl.multiple_of(gx * 32, 32), 32), :]
    esum[...] = own + hsum[0] + hsum[1] + hsum[2]

    @pl.when(gz > 0)
    def _():
        to_surface = pltpu.make_async_remote_copy(
            src_ref=esum, dst_ref=ksum.at[gz - 1], send_sem=f3s, recv_sem=f3r.at[gz - 1],
            device_id=(gx, gy, 0), device_id_type=MESH,
        )
        to_surface.start()

    got(r2x, r2y)

    @pl.when(has_xp)
    def _():
        unpack_x(xh2, [p1, m1], CX)

    every(lambda z: s2(z, yh2), 1, CZ - 1)

    lo3 = V1 + MA0
    pack_x(xa3, lo3, 0)
    pack_x(xb3, lo3 + [A0[0]], CX - 1)
    r3x = [x_down(xa3, xh3), x_up(xb3, xl3)]
    pack_y(ys3, lo3 + [A0[1]])
    r3y = [y_down(ys3, yh3), y_up(ys3, yl3)]
    go(*r3y)

    for one in zpart + zpm:
        one.flush()
    got(*zraw, *zpm)

    surface = gz == 0
    r5x = [
        link("x", xa5, xh5, (gx - 1, gy, gz), surface & has_xm, surface & has_xp),
        link("x", xb5, xl5, (gx + 1, gy, gz), surface & has_xp, surface & has_xm),
    ]
    r5y = [
        link("y", ys5, yh5, (gx, gy - 1, gz), surface & has_ym, surface & has_yp),
        link("y", ys5, yl5, (gx, gy + 1, gz), surface & has_yp, surface & has_ym),
    ]

    @pl.when(surface)
    def _():
        for other in range(1, NGZ):
            pltpu.make_async_remote_copy(
                src_ref=esum, dst_ref=ksum.at[other - 1], send_sem=f3s, recv_sem=f3r.at[other - 1],
                device_id=(gx, gy, 1), device_id_type=MESH,
            ).wait_recv()
        total = esum[...]
        for other in range(1, NGZ):
            total = total + ksum[other - 1]
        esum[...] = total
        w = ld(A1[2], 0) + total[CX:2 * CX]
        st(A1[2], 0, w)
        w = w * ld(md, 0)
        st(MA[2], 0, w)
        pack_rows(xa5, [(MA[2], 0)], 0)
        pack_rows(xb5, [(MA[2], 0)], CX - 1)
        ys5[...] = pltpu.roll(w, 11, 1)

    go(*r5x, *r5y)


    @pl.when(has_zm)
    def _():
        for c in range(3):
            st(V0[c], -1, zl[c])
            st(MA[c], -1, zl[6] * zl[3 + c])
        st(A1[2], -1, zl[5])

    @pl.when(has_zp)
    def _():
        for c in range(3):
            st(V0[c], CZ, zu[c])
            st(MA[c], CZ, zu[6] * zu[3 + c])
        st(p1, CZ, zu[13] - ld(V0[2], CZ - 1))
        st(m1, CZ, zu[14] + 0.25 * ld(A1[2], CZ - 1))

    some(lambda z: s1(z, c1), rim)
    x6 = [(p1, 0), (m1, 0), (m1, 1), (A1[2], CZ - 1)]
    pack_rows(xa6, x6, 0)
    r6x = x_down(xa6, xh6)
    go(r6x)
    pack_layers(ys6, [p1, m1, A1[2]], rim)
    r6y = y_down(ys6, yh6)
    go(r6y)
    go(*r3x)

    got(r6x, r6y, *r5x, *r5y)
    @pl.when(surface & has_xp)
    def _():
        unpack_rows(xh5, [(MA[2], 0)], CX)

    @pl.when(surface & has_xm)
    def _():
        unpack_rows(xl5, [(MA[2], 0)], -1)

    @pl.when(surface & has_yp)
    def _():
        yh1[0] = jnp.where(lane == 11, yh5[...], yh1[0])

    @pl.when(surface & has_ym)
    def _():
        yl1[0] = jnp.where(lane == 10, yl5[...], yl1[0])

    @pl.when(surface)
    def _():
        merge(c1, yl1, yh1, (0,))
        lm[2, 0], _ = lap(MA[2], 0, c1, 5)


    @pl.when(has_xp)
    def _():
        unpack_rows(xh6, x6, CX)

    some(lambda z: s2(z, yh6), rim)
    got(*zpart)

    @pl.when(surface)
    def _():
        w = ld(A0[2], 0) + esum[0:CX, :]
        st(A0[2], 0, w)
        st(MA0[2], 0, w * ld(md, 0))

    @pl.when(has_zm)
    def _():
        g = zl[6]
        extra_v, extra_a = ld(p1, 0), ld(m1, 0)
        for c in range(3):
            v = g * ld(V0[c], 0)
            a = 0.25 * ld(MA[c], 0)
            if c == 2:
                v, a = v + extra_v, a - extra_a
            st(V1[c], -1, zl[7 + c] + 0.25 * v)
            a = zl[10 + c] + a
            st(A0[c], -1, a)
            st(MA0[c], -1, g * a)

    @pl.when(has_zp)
    def _():
        g = zu[6]
        top = CZ - 1
        q, w = ld(V0[2], top), ld(A1[2], top)
        gq = (ld(V0[2], top, 1) - q, yhi(q, yh1, top, 2) - q, -q)
        gw = (ld(A1[2], top, 1) - w, yhi(w, yh6, top, 2) - w, -w)
        for c in range(3):
            st(V1[c], CZ, zu[7 + c] + 0.25 * (g * ld(V0[c], top) - gq[c]))
            a = zu[10 + c] + 0.25 * (ld(MA[c], top) - gw[c])
            st(A0[c], CZ, a)
            st(MA0[c], CZ, g * a)

    x7 = [(ref, z) for ref in lo3 for z in (0, 1, CZ - 1)]
    x7up = x7 + [(A0[0], z) for z in (0, 1, CZ - 1, CZ)]
    pack_rows(xa7, x7, 0)
    pack_rows(xb7, x7up, CX - 1)
    r7x = [x_down(xa7, xh7), x_up(xb7, xl7)]
    go(*r7x)
    edges = (0, 1, 2, CZ - 2, CZ - 1)
    pack_layers(ys7, lo3 + [A0[1]], edges, last=A0[1])
    r7y = [y_down(ys7, yh7), y_up(ys7, yl7)]
    go(*r7y)
    got(*r3x, *r3y)

    @pl.when(has_xp)
    def _():
        unpack_x(xh3, lo3, CX)

    @pl.when(has_xm)
    def _():
        unpack_x(xl3, lo3 + [A0[0]], -1)

    merge(c3, yl3, yh3)
    every(lambda z: s3(z, c3), 3, CZ - 2)
    pack_x(xa4, [m0], 0)
    r4x = x_down(xa4, xh4)
    go(r4x)
    pack_y(ys4, [m0])
    r4y = y_down(ys4, yh4)
    go(r4y)

    got(*r7x, *r7y)

    @pl.when(has_xp)
    def _():
        unpack_rows(xh7, x7, CX)

    @pl.when(has_xm)
    def _():
        unpack_rows(xl7, x7up, -1)

    merge(c7, yl7, yh7)
    some(lambda z: s3(z, c7), edges)

    @pl.when(has_zp)
    def _():
        x, y, w = (ld(r, CZ) for r in A0)
        low = jnp.where(lane == 0, pltpu.roll(yl7[3], 2, 1), pltpu.roll(y, 1, 1))
        d = (x - ld(A0[0], CZ, -1)) + (y - low) + (w - ld(A0[2], CZ - 1))
        st(m0, CZ, ld(m1, CZ) - 0.25 * d)

    x8 = [(m0, z) for z in edges + (CZ - 3,)]
    pack_rows(xa8, x8, 0)
    r8x = x_down(xa8, xh8)
    go(r8x)
    pack_layers(ys8, [m0], edges + (CZ - 3,))
    r8y = y_down(ys8, yh8)
    go(r8y)
    got(r4x, r4y)

    @pl.when(has_xp)
    def _():
        unpack_x(xh4, [m0], CX)

    every(lambda z: s4(z, yh4), 3, CZ - 3)
    early = store(3, CZ - 6, 0)
    got(r8x, r8y)

    @pl.when(has_xp)
    def _():
        unpack_rows(xh8, x8, CX)

    some(lambda z: s4(z, yh8), (0, 1, 2, CZ - 3, CZ - 2, CZ - 1))
    late = store(0, 3, 1) + store(CZ - 3, 3, 2)
    for one in links:
        if one not in zpart and one not in zpm:
            one.flush()
    for copy in stage1 + stage2:
        copy.wait_send()

    @pl.when(gz > 0)
    def _():
        pltpu.make_async_remote_copy(
            src_ref=esum, dst_ref=ksum.at[gz - 1], send_sem=f3s, recv_sem=f3r.at[gz - 1],
            device_id=(gx, gy, 0), device_id_type=MESH,
        ).wait_send()

    for copy in early + late:
        copy.wait()


def hand_out(a, b, c, oa, ob, oc, held, sem_in, sem_out):
    pieces = [(a.at[k], oa.at[k]) for k in range(3)] + [(b, ob), (c, oc)]
    ins = [pltpu.make_async_copy(p[0], held.at[k], sem_in.at[k]) for k, p in enumerate(pieces)]
    outs = [pltpu.make_async_copy(held.at[k], p[1], sem_out.at[k]) for k, p in enumerate(pieces)]
    for copy in ins:
        copy.start()
    for first, second in zip(ins, outs):
        first.wait()
        second.start()
    for copy in outs:
        copy.wait()


def shards(vel, pres, modulus, avel, apres, svals, sowner, sline, sstep):
    vector = pltpu.VMEM((3, ROWS, CY), F32)
    scalar = pltpu.VMEM((ROWS, CY), F32)
    flat3 = pltpu.VMEM((3, CZ, CX, CY), F32)
    flat = pltpu.VMEM((CZ, CX, CY), F32)
    pack = pltpu.VMEM((4, CX, CY), F32)
    plane = pltpu.VMEM((CX, CY), F32)
    ints = pltpu.VMEM((1, 32), jnp.int32)

    def lines(n):
        return pltpu.VMEM((n, CY), F32)

    def dma(n):
        return pltpu.SemaphoreType.DMA((n,))

    anywhere = pl.BlockSpec(memory_space=pl.ANY)
    inner = pl.pallas_call(
        body,
        out_shape=(
            jax.ShapeDtypeStruct((3, CZ, CX, CY), F32),
            jax.ShapeDtypeStruct((CZ, CX, CY), F32),
            jax.ShapeDtypeStruct((CZ, CX, CY), F32),
        ),
        in_specs=[anywhere] * 9,
        out_specs=(anywhere,) * 3,
        scratch_shapes=[
            vector, vector, vector, scalar, scalar, scalar, vector, vector, vector, scalar,
            flat, flat, flat3, flat3, flat3, flat, flat3,
            pack, pack, pack, pack, pack, pack, pack, pack, pack, pack,
            pack, pack, pack, pack, pack, lines(24), lines(24), lines(24), lines(24), lines(8), lines(8),
            plane, plane, plane, pack, pack, pack, pack, pack, pack, pack,
            lines(6 * CZ), lines(7 * CZ), lines(6 * CZ), lines(7 * CZ),
            lines(2 * CZ), lines(2 * CZ),
            lines(6 * CZ), lines(7 * CZ), lines(6 * CZ), lines(7 * CZ),
            lines(CZ), lines(CZ),
            lines(8), lines(8), lines(8), lines(8), lines(8), lines(8),
            lines(24), lines(24), lines(24), lines(24), lines(8), lines(8),
            lines(32), ints, ints, ints,
            pltpu.VMEM((13, CX, CY), F32), pltpu.VMEM((15, CX, CY), F32),
            lines(256), lines(256), lines(CY), pltpu.VMEM((3, 32, CY), F32), lines(32),
            pltpu.VMEM((NGZ - 1, 32, CY), F32),
            dma(9), dma(9), dma(15), dma(15), dma(13), dma(13), dma(12), dma(12),
            dma(NGY - 1), dma(NGY - 1), dma(NGX - 1), dma(NGX - 1),
            pltpu.SemaphoreType.DMA, dma(NGZ - 1),
        ],
        compiler_params=pltpu.CompilerParams(
            collective_id=0, has_side_effects=True, vmem_limit_bytes=62 * 2**20
        ),
        cost_estimate=pl.CostEstimate(flops=20_000_000, bytes_accessed=3_670_016, transcendentals=0),
        name="adjoint",
    )(vel, pres, modulus, avel, apres, svals, sowner.reshape(1, 32), sline.reshape(1, 32), sstep.reshape(1, 32))
    return pl.pallas_call(
        hand_out,
        out_shape=[jax.ShapeDtypeStruct(a.shape, F32) for a in inner],
        in_specs=[anywhere] * 3,
        out_specs=[anywhere] * 3,
        scratch_shapes=[pltpu.VMEM((5, CZ, CX, CY), F32), dma(5), dma(5)],
        compiler_params=pltpu.CompilerParams(vmem_limit_bytes=62 * 2**20),
        name="handout",
    )(*inner)


def solution(mesh):
    return jax.shard_map(
        shards,
        mesh=mesh,
        in_specs=(
            P(None, "gz", "gx", "gy"),
            P("gz", "gx", "gy"),
            P("gz", "gx", "gy"),
            P(None, "gz", "gx", "gy"),
            P("gz", "gx", "gy"),
            P(("gx", "gy", "gz"), None),
            P(("gx", "gy", "gz"), None),
            P(("gx", "gy", "gz")),
            P(("gx", "gy", "gz")),
        ),
        out_specs=(P(None, "gz", "gx", "gy"), P("gz", "gx", "gy"), P("gz", "gx", "gy")),
        check_vma=False,
    )
```

time: 62.8 us -> 45.5 us (0.72)
  the two profiles are of different devices: /device:TPU:25 before, /device:TPU:1 now
where the time goes in v2:
time: 45.5 us; the launch traced here: 45.2 us
  Pallas kernels  44.6 us (98%)
  between operations  0.64 us (1%)
    pallas_call x1, Pallas kernels, shards(): pl.pallas_call(body, out_shape=(jax.ShapeDtypeStruct((3, CZ, CX, CY), F32...  42.5 us
    pallas_call x1, Pallas kernels, shards(): pl.pallas_call(hand_out, out_shape=[jax.ShapeDtypeStruct(a.shape, F32) fo...  2.08 us

profile of v2, /device:TPU:1, one launch (start us, length us, event | category | flops | bytes accessed | tf_op | source)
XLA Modules:
  0.0 45.2 jit_solution(10529307354276039582)
XLA Ops:
  0.6 42.5 %adjoint.1 = (f32[3,32,16,128]{3,2,1,0:T(8,128)}, f32[32,16,128]{2,1,0:T(8,128)}, f32[32,16,128]{2,1,0:T(8,128)}) custom-call(f32[3,32,16,128]{3,2,1,0:T(8,128)} %vel.1, f32[32,16,128]{2,1,0:T(8,128)} %pres.1, f32[32,16,128]{2,1,0:T(8,128)} %modulus.1, f32[3,32,16,128]{3,2,1,0:T(8,128)} %avel.1, f32[32,16,128]{2,1,0:T(8,128)} %apres.1, f32[32,128]{1,0:T(8,128)} %svals_h.1, ...), custom_call_target="tpu_custom_call" | custom-call | flops 20000000 | bytes 3670016 | tf_op jit(solution)/shard_map/adjoint/pallas_call | solution.py:740
  43.1 2.1 %handout.1 = (f32[3,32,16,128]{3,2,1,0:T(8,128)}, f32[32,16,128]{2,1,0:T(8,128)}, f32[32,16,128]{2,1,0:T(8,128)}) custom-call(f32[3,32,16,128]{3,2,1,0:T(8,128)} %get-tuple-element.6.a, f32[32,16,128]{2,1,0:T(8,128)} %get-tuple-element.7.b, f32[32,16,128]{2,1,0:T(8,128)} %get-tuple-element.8.c), custom_call_target="tpu_custom_call" | custom-call | tf_op jit(solution)/shard_map/handout/pallas_call | solution.py:775

commit v3 on v2

--- a/solution.py
+++ b/solution.py
@@ -27,7 +27,7 @@
     xa1, xb1, xh1, xl1, xa2, xh2, xa3, xb3, xh3, xl3, xa4, xh4,
     xa5, xb5, xh5, xl5, xa6, xh6, xa7, xb7, xh7, xl7, xa8, xh8,
     svals, sowner, sline, sstep,
-    zl, zu, cs, gath, dense, hsum, esum, ksum,
+    zl, zu, to_up, to_down, from_low, from_high, cs, gath, dense, hsum, esum, ksum,
     in_sem, out_sem, xs_sem, xr_sem, ys_sem, yr_sem, zs_sem, zr_sem,
     f1s, f1r, f2s, f2r, f3s, f3r,
 ):
@@ -337,12 +337,12 @@
     r1y = [y_down(ys1, yh1), y_up(ys1, yl1)]
     r1x = [x_down(xa1, xh1), x_up(xb1, xl1)]
     zraw = [
-        z_up(vel.at[:, CZ - 1], zl.at[0:3]),
-        z_down(vel.at[:, 0], zu.at[0:3]),
         z_up(avel.at[:, CZ - 1], zl.at[3:6]),
         z_down(avel.at[:, 0], zu.at[3:6]),
         z_up(modulus.at[CZ - 1], zl.at[6]),
         z_down(modulus.at[0], zu.at[6]),
+        z_up(vel.at[:, CZ - 1], zl.at[0:3]),
+        z_down(vel.at[:, 0], zu.at[0:3]),
     ]
     go(*r9x, *r1y, *zraw)
     pack_x(xa1, lo1, 0)
@@ -405,26 +405,10 @@
     pack_layers(ys9, [p1, m1], (0, CZ - 1))
     r9y = y_down(ys9, yh9)
     zpm = [
-        z_down(p1.at[pl.ds(PITCH + 8, CX)], zu.at[13]),
-        z_down(m1.at[pl.ds(PITCH + 8, CX)], zu.at[14]),
+        z_down(p1.at[pl.ds(PITCH + 8, CX)], zu.at[10]),
+        z_down(m1.at[pl.ds(PITCH + 8, CX)], zu.at[11]),
     ]
     go(r9y, *zpm)
-    got(r10x, r9y)
-
-    @pl.when(has_xp)
-    def _():
-        unpack_rows(xh10, x10, CX)
-
-    some(lambda z: s2(z, yh9), (0, CZ - 1))
-    first, final = pl.ds(PITCH + 8, CX), pl.ds(CZ * PITCH + 8, CX)
-    zpart = [
-        z_up(v1.at[:, final], zl.at[7:10]),
-        z_down(v1.at[:, first], zu.at[7:10]),
-        z_up(a0.at[:, final], zl.at[10:13]),
-        z_down(a0.at[:, first], zu.at[10:13]),
-    ]
-    go(*zpart)
-
     for copy in stage1:
         copy.wait_recv()
     rows = gath[...]
@@ -448,6 +432,20 @@
         )
         stage2[-1].start()
 
+    got(r10x, r9y)
+
+    @pl.when(has_xp)
+    def _():
+        unpack_rows(xh10, x10, CX)
+
+    some(lambda z: s2(z, yh9), (0, CZ - 1))
+    first, final = pl.ds(PITCH + 8, CX), pl.ds(CZ * PITCH + 8, CX)
+    zpart = [
+        z_up(a0.at[:, final], zl.at[7:10]),
+        z_down(a0.at[:, first], zu.at[7:10]),
+    ]
+    go(*zpart)
+
     got(*r1x)
 
     @pl.when(has_xp)
@@ -491,6 +489,7 @@
     pack_x(xa3, lo3, 0)
     pack_x(xb3, lo3 + [A0[0]], CX - 1)
     r3x = [x_down(xa3, xh3), x_up(xb3, xl3)]
+    go(*r3x)
     pack_y(ys3, lo3 + [A0[1]])
     r3y = [y_down(ys3, yh3), y_up(ys3, yl3)]
     go(*r3y)
@@ -543,8 +542,8 @@
         for c in range(3):
             st(V0[c], CZ, zu[c])
             st(MA[c], CZ, zu[6] * zu[3 + c])
-        st(p1, CZ, zu[13] - ld(V0[2], CZ - 1))
-        st(m1, CZ, zu[14] + 0.25 * ld(A1[2], CZ - 1))
+        st(p1, CZ, zu[10] - ld(V0[2], CZ - 1))
+        st(m1, CZ, zu[11] + 0.25 * ld(A1[2], CZ - 1))
 
     some(lambda z: s1(z, c1), rim)
     x6 = [(p1, 0), (m1, 0), (m1, 1), (A1[2], CZ - 1)]
@@ -554,7 +553,6 @@
     pack_layers(ys6, [p1, m1, A1[2]], rim)
     r6y = y_down(ys6, yh6)
     go(r6y)
-    go(*r3x)
 
     got(r6x, r6y, *r5x, *r5y)
     @pl.when(surface & has_xp)
@@ -584,6 +582,11 @@
         unpack_rows(xh6, x6, CX)
 
     some(lambda z: s2(z, yh6), rim)
+
+    to_up[...] = sum(ld(V1[c], CZ - 1) * zu[3 + c] for c in range(3))
+    to_down[...] = sum(ld(V1[c], 0) * zl[3 + c] for c in range(3))
+    zshare = [z_up(to_up, from_low), z_down(to_down, from_high)]
+    go(*zshare)
     got(*zpart)
 
     @pl.when(surface)
@@ -595,14 +598,9 @@
     @pl.when(has_zm)
     def _():
         g = zl[6]
-        extra_v, extra_a = ld(p1, 0), ld(m1, 0)
+        extra = ld(m1, 0)
         for c in range(3):
-            v = g * ld(V0[c], 0)
-            a = 0.25 * ld(MA[c], 0)
-            if c == 2:
-                v, a = v + extra_v, a - extra_a
-            st(V1[c], -1, zl[7 + c] + 0.25 * v)
-            a = zl[10 + c] + a
+            a = zl[7 + c] + 0.25 * ld(MA[c], 0) - (extra if c == 2 else 0.0)
             st(A0[c], -1, a)
             st(MA0[c], -1, g * a)
 
@@ -610,12 +608,10 @@
     def _():
         g = zu[6]
         top = CZ - 1
-        q, w = ld(V0[2], top), ld(A1[2], top)
-        gq = (ld(V0[2], top, 1) - q, yhi(q, yh1, top, 2) - q, -q)
+        w = ld(A1[2], top)
         gw = (ld(A1[2], top, 1) - w, yhi(w, yh6, top, 2) - w, -w)
         for c in range(3):
-            st(V1[c], CZ, zu[7 + c] + 0.25 * (g * ld(V0[c], top) - gq[c]))
-            a = zu[10 + c] + 0.25 * (ld(MA[c], top) - gw[c])
+            a = zu[7 + c] + 0.25 * (ld(MA[c], top) - gw[c])
             st(A0[c], CZ, a)
             st(MA0[c], CZ, g * a)
 
@@ -690,6 +686,16 @@
         unpack_rows(xh8, x8, CX)
 
     some(lambda z: s4(z, yh8), (0, 1, 2, CZ - 3, CZ - 2, CZ - 1))
+    got(*zshare)
+
+    @pl.when(has_zm)
+    def _():
+        sh[0] = sh[0] + 0.25 * from_low[...]
+
+    @pl.when(has_zp)
+    def _():
+        sh[CZ - 1] = sh[CZ - 1] + 0.25 * from_high[...]
+
     late = store(0, 3, 1) + store(CZ - 3, 3, 2)
     for one in links:
         if one not in zpart and one not in zpm:
@@ -759,7 +765,8 @@
             lines(8), lines(8), lines(8), lines(8), lines(8), lines(8),
             lines(24), lines(24), lines(24), lines(24), lines(8), lines(8),
             lines(32), ints, ints, ints,
-            pltpu.VMEM((13, CX, CY), F32), pltpu.VMEM((15, CX, CY), F32),
+            pltpu.VMEM((10, CX, CY), F32), pltpu.VMEM((12, CX, CY), F32),
+            plane, plane, plane, plane,
             lines(256), lines(256), lines(CY), pltpu.VMEM((3, 32, CY), F32), lines(32),
             pltpu.VMEM((NGZ - 1, 32, CY), F32),
             dma(9), dma(9), dma(15), dma(15), dma(13), dma(13), dma(12), dma(12),

time: 45.5 us -> 42.5 us (0.934)
  Pallas kernels: 44.6 us -> 41.8 us
    pallas_call x1, Pallas kernels: 42.5 us -> 39.7 us  [shards(): pl.pallas_call(body, out_shape=(jax.ShapeDtypeStruct((3, CZ, CX, CY), F32...]
where the time goes in v3:
time: 42.5 us; the launch traced here: 42.4 us
  Pallas kernels  41.8 us (98%)
  between operations  0.64 us (2%)
    pallas_call x1, Pallas kernels, shards(): pl.pallas_call(body, out_shape=(jax.ShapeDtypeStruct((3, CZ, CX, CY), F32...  39.7 us
    pallas_call x1, Pallas kernels, shards(): pl.pallas_call(hand_out, out_shape=[jax.ShapeDtypeStruct(a.shape, F32) fo...  2.08 us

profile of v3, /device:TPU:1, one launch (start us, length us, event | category | flops | bytes accessed | tf_op | source)
XLA Modules:
  0.0 42.4 jit_solution(1482631606209926006)
XLA Ops:
  0.6 39.7 %adjoint.1 = (f32[3,32,16,128]{3,2,1,0:T(8,128)}, f32[32,16,128]{2,1,0:T(8,128)}, f32[32,16,128]{2,1,0:T(8,128)}) custom-call(f32[3,32,16,128]{3,2,1,0:T(8,128)} %vel.1, f32[32,16,128]{2,1,0:T(8,128)} %pres.1, f32[32,16,128]{2,1,0:T(8,128)} %modulus.1, f32[3,32,16,128]{3,2,1,0:T(8,128)} %avel.1, f32[32,16,128]{2,1,0:T(8,128)} %apres.1, f32[32,128]{1,0:T(8,128)} %svals_h.1, ...), custom_call_target="tpu_custom_call" | custom-call | flops 20000000 | bytes 3670016 | tf_op jit(solution)/shard_map/adjoint/pallas_call | solution.py:746
  40.3 2.1 %handout.1 = (f32[3,32,16,128]{3,2,1,0:T(8,128)}, f32[32,16,128]{2,1,0:T(8,128)}, f32[32,16,128]{2,1,0:T(8,128)}) custom-call(f32[3,32,16,128]{3,2,1,0:T(8,128)} %get-tuple-element.6.a, f32[32,16,128]{2,1,0:T(8,128)} %get-tuple-element.7.b, f32[32,16,128]{2,1,0:T(8,128)} %get-tuple-element.8.c), custom_call_target="tpu_custom_call" | custom-call | tf_op jit(solution)/shard_map/handout/pallas_call | solution.py:782

commit v4 on v3

--- a/solution.py
+++ b/solution.py
@@ -714,16 +714,12 @@
         copy.wait()
 
 
-def hand_out(a, b, c, oa, ob, oc, held, sem_in, sem_out):
+def hand_out(a, b, c, oa, ob, oc, sem):
     pieces = [(a.at[k], oa.at[k]) for k in range(3)] + [(b, ob), (c, oc)]
-    ins = [pltpu.make_async_copy(p[0], held.at[k], sem_in.at[k]) for k, p in enumerate(pieces)]
-    outs = [pltpu.make_async_copy(held.at[k], p[1], sem_out.at[k]) for k, p in enumerate(pieces)]
-    for copy in ins:
+    copies = [pltpu.make_async_copy(p[0], p[1], sem.at[k]) for k, p in enumerate(pieces)]
+    for copy in copies:
         copy.start()
-    for first, second in zip(ins, outs):
-        first.wait()
-        second.start()
-    for copy in outs:
+    for copy in copies:
         copy.wait()
 
 
@@ -743,6 +739,12 @@
         return pltpu.SemaphoreType.DMA((n,))
 
     anywhere = pl.BlockSpec(memory_space=pl.ANY)
+    sowner, sline, sstep = (a.reshape(1, 32) for a in (sowner, sline, sstep))
+    operands = [
+        pltpu.with_memory_space_constraint(a, pltpu.HBM)
+        for a in (vel, pres, modulus, avel, apres, svals, sowner, sline, sstep)
+    ]
+    vel, pres, modulus, avel, apres, svals, sowner, sline, sstep = operands
     inner = pl.pallas_call(
         body,
         out_shape=(
@@ -774,18 +776,18 @@
             pltpu.SemaphoreType.DMA, dma(NGZ - 1),
         ],
         compiler_params=pltpu.CompilerParams(
-            collective_id=0, has_side_effects=True, vmem_limit_bytes=62 * 2**20
+            collective_id=0, has_side_effects=True, vmem_limit_bytes=40 * 2**20
         ),
         cost_estimate=pl.CostEstimate(flops=20_000_000, bytes_accessed=3_670_016, transcendentals=0),
         name="adjoint",
-    )(vel, pres, modulus, avel, apres, svals, sowner.reshape(1, 32), sline.reshape(1, 32), sstep.reshape(1, 32))
+    )(vel, pres, modulus, avel, apres, svals, sowner, sline, sstep)
     return pl.pallas_call(
         hand_out,
         out_shape=[jax.ShapeDtypeStruct(a.shape, F32) for a in inner],
-        in_specs=[anywhere] * 3,
-        out_specs=[anywhere] * 3,
-        scratch_shapes=[pltpu.VMEM((5, CZ, CX, CY), F32), dma(5), dma(5)],
-        compiler_params=pltpu.CompilerParams(vmem_limit_bytes=62 * 2**20),
+        in_specs=[pl.BlockSpec(memory_space=pltpu.VMEM)] * 3,
+        out_specs=[pl.BlockSpec(memory_space=pltpu.HBM)] * 3,
+        scratch_shapes=[dma(5)],
+        compiler_params=pltpu.CompilerParams(vmem_limit_bytes=16 * 2**20),
         name="handout",
     )(*inner)
 

time: 42.5 us -> 41.2 us (0.969)
  Pallas kernels: 41.8 us -> 40.5 us
    pallas_call x1, Pallas kernels: 2.08 us -> 1.09 us  [shards(): pl.pallas_call(hand_out, out_shape=[jax.ShapeDtypeStruct(a.shape, F32) fo...]
where the time goes in v4:
time: 41.2 us; the launch traced here: 41.1 us
  Pallas kernels  40.5 us (98%)
  between operations  0.64 us (2%)
    pallas_call x1, Pallas kernels, shards(): pl.pallas_call(body, out_shape=(jax.ShapeDtypeStruct((3, CZ, CX, CY), F32...  39.4 us
    pallas_call x1, Pallas kernels, shards(): pl.pallas_call(hand_out, out_shape=[jax.ShapeDtypeStruct(a.shape, F32) fo...  1.09 us

profile of v4, /device:TPU:1, one launch (start us, length us, event | category | flops | bytes accessed | tf_op | source)
XLA Modules:
  0.0 41.1 jit_solution(3022208334457400029)
XLA Ops:
  0.6 39.4 %adjoint.1 = (f32[3,32,16,128]{3,2,1,0:T(8,128)S(1)}, f32[32,16,128]{2,1,0:T(8,128)S(1)}, f32[32,16,128]{2,1,0:T(8,128)S(1)}) custom-call(f32[3,32,16,128]{3,2,1,0:T(8,128)} %vel.1, f32[32,16,128]{2,1,0:T(8,128)} %pres.1, f32[32,16,128]{2,1,0:T(8,128)} %modulus.1, f32[3,32,16,128]{3,2,1,0:T(8,128)} %avel.1, f32[32,16,128]{2,1,0:T(8,128)} %apres.1, ...), custom_call_target="tpu_custom_call" | custom-call | flops 20000000 | bytes 3670016 | tf_op jit(solution)/shard_map/adjoint/pallas_call | solution.py:748
  40.0 1.1 %handout.1 = (f32[3,32,16,128]{3,2,1,0:T(8,128)}, f32[32,16,128]{2,1,0:T(8,128)}, f32[32,16,128]{2,1,0:T(8,128)}) custom-call(f32[3,32,16,128]{3,2,1,0:T(8,128)S(1)} %get-tuple-element.6.a, f32[32,16,128]{2,1,0:T(8,128)S(1)} %get-tuple-element.7.b, f32[32,16,128]{2,1,0:T(8,128)S(1)} %get-tuple-element.8.c), custom_call_target="tpu_custom_call" | custom-call | tf_op jit(solution)/shard_map/handout/pallas_call | solution.py:784

commit v5 on v4

--- a/solution.py
+++ b/solution.py
@@ -12,7 +12,7 @@
 LAYERS = CZ + 2
 ROWS = LAYERS * PITCH
 NGX, NGY, NGZ = 4, 8, 8
-UNROLL = 4
+UNROLL = 8
 HIGH = lax.Precision.HIGHEST
 
 
@@ -103,18 +103,21 @@
 
     zeros_layer = jnp.zeros((PITCH, CY), F32)
     zeros_rows = jnp.zeros((LAYERS, CY), F32)
+    for ref in V1:
+        ref[pl.ds(7, LAYERS, stride=PITCH), :] = zeros_rows
+        ref[pl.ds(24, LAYERS, stride=PITCH), :] = zeros_rows
     for ref in V0 + A1 + MA + V1 + A0 + MA0 + [p1, m1, m0]:
         ref[0:PITCH, :] = zeros_layer
         ref[ROWS - PITCH:ROWS, :] = zeros_layer
 
     @pl.when(jnp.logical_not(has_xm))
     def _():
-        for ref in V0 + [A1[0]] + MA + V1 + [A0[0]] + MA0:
+        for ref in V0 + [A1[0]] + MA + [A0[0]] + MA0:
             ref[pl.ds(7, LAYERS, stride=PITCH), :] = zeros_rows
 
     @pl.when(jnp.logical_not(has_xp))
     def _():
-        for ref in V0 + MA + [A1[2]] + V1 + MA0 + [p1, m1, m0]:
+        for ref in V0 + MA + [A1[2]] + MA0 + [p1, m1, m0]:
             ref[pl.ds(24, LAYERS, stride=PITCH), :] = zeros_rows
 
     def ld(ref, z, dx=0):
@@ -234,6 +237,20 @@
     def unpack_x(src, fields, x):
         for i, ref in enumerate(fields):
             ref[pl.ds(PITCH + 8 + x, CZ, stride=PITCH), :] = src[i * CZ:(i + 1) * CZ, :]
+
+    def weigh_x(to, ref, x):
+        for c in range(3):
+            to[c][pl.ds(PITCH + 8 + x, CZ, stride=PITCH), :] = face(md, x) * face(ref[c], x)
+
+    def row(ref, z, x):
+        at = (z + 1) * PITCH + 8 + x
+        return ref[at:at + 1, :]
+
+    def weigh_rows(to, ref, layers, x):
+        for z in layers:
+            at = (z + 1) * PITCH + 8 + x
+            for c in range(3):
+                to[c][at:at + 1, :] = row(md, z, x) * row(ref[c], z, x)
 
     def rows_of(pairs, x):
         return [(ref, (z + 1) * PITCH + 8 + x) for ref, z in pairs]
@@ -325,10 +342,10 @@
     every(weight)
     lo1 = V0 + MA
     rim = (0, 1, CZ - 1)
-    x9 = [(ref, z) for ref in lo1 for z in rim]
-    x9up = x9 + [(A1[0], z) for z in rim]
+    wide1 = V0 + A1 + [md]
+    x9 = [(ref, z) for ref in wide1 for z in rim]
     pack_rows(xa9, x9, 0)
-    pack_rows(xb9, x9up, CX - 1)
+    pack_rows(xb9, x9, CX - 1)
     pack_y(ys1, lo1 + [A1[1]])
 
     pl.semaphore_wait(barrier, expected)
@@ -345,8 +362,8 @@
         z_down(vel.at[:, 0], zu.at[0:3]),
     ]
     go(*r9x, *r1y, *zraw)
-    pack_x(xa1, lo1, 0)
-    pack_x(xb1, lo1 + [A1[0]], CX - 1)
+    pack_x(xa1, wide1, 0)
+    pack_x(xb1, wide1, CX - 1)
     go(*r1x)
 
     for copy in sensors:
@@ -391,10 +408,12 @@
     @pl.when(has_xp)
     def _():
         unpack_rows(xh9, x9, CX)
+        weigh_rows(MA, A1, rim, CX)
 
     @pl.when(has_xm)
     def _():
-        unpack_rows(xl9, x9up, -1)
+        unpack_rows(xl9, x9, -1)
+        weigh_rows(MA, A1, rim, -1)
 
     merge(c1, yl1, yh1)
     some(lambda z: s1(z, c1), rim)
@@ -450,13 +469,30 @@
 
     @pl.when(has_xp)
     def _():
-        unpack_x(xh1, lo1, CX)
+        unpack_x(xh1, wide1, CX)
+        weigh_x(MA, A1, CX)
 
     @pl.when(has_xm)
     def _():
-        unpack_x(xl1, lo1 + [A1[0]], -1)
-
-    every(lambda z: s1(z, c1), 2, CZ - 1)
+        unpack_x(xl1, wide1, -1)
+        weigh_x(MA, A1, -1)
+
+    every(lambda z: s1(z, c1), 2, 14)
+
+    for copy in stage2:
+        copy.wait_recv()
+    own = dense[pl.ds(pl.multiple_of(gx * 32, 32), 32), :]
+    esum[...] = own + hsum[0] + hsum[1] + hsum[2]
+
+    @pl.when(gz > 0)
+    def _():
+        to_surface = pltpu.make_async_remote_copy(
+            src_ref=esum, dst_ref=ksum.at[gz - 1], send_sem=f3s, recv_sem=f3r.at[gz - 1],
+            device_id=(gx, gy, 0), device_id_type=MESH,
+        )
+        to_surface.start()
+
+    every(lambda z: s1(z, c1), 14, CZ - 1)
     pack_x(xa2, [p1, m1], 0)
     r2x = x_down(xa2, xh2)
     go(r2x)
@@ -464,19 +500,6 @@
     r2y = y_down(ys2, yh2)
     go(r2y)
 
-    for copy in stage2:
-        copy.wait_recv()
-    own = dense[pl.ds(pl.multiple_of(gx * 32, 32), 32), :]
-    esum[...] = own + hsum[0] + hsum[1] + hsum[2]
-
-    @pl.when(gz > 0)
-    def _():
-        to_surface = pltpu.make_async_remote_copy(
-            src_ref=esum, dst_ref=ksum.at[gz - 1], send_sem=f3s, recv_sem=f3r.at[gz - 1],
-            device_id=(gx, gy, 0), device_id_type=MESH,
-        )
-        to_surface.start()
-
     got(r2x, r2y)
 
     @pl.when(has_xp)
@@ -486,8 +509,10 @@
     every(lambda z: s2(z, yh2), 1, CZ - 1)
 
     lo3 = V1 + MA0
-    pack_x(xa3, lo3, 0)
-    pack_x(xb3, lo3 + [A0[0]], CX - 1)
+    pack_x(xa3, A0, 0)
+    pack_x(xb3, A0, CX - 1)
+    xa3[3 * CZ:, :] = sum(face(V1[c], 0) * face(A1[c], -1) for c in range(3))
+    xb3[3 * CZ:, :] = sum(face(V1[c], CX - 1) * face(A1[c], CX) for c in range(3))
     r3x = [x_down(xa3, xh3), x_up(xb3, xl3)]
     go(*r3x)
     pack_y(ys3, lo3 + [A0[1]])
@@ -523,8 +548,8 @@
         st(A1[2], 0, w)
         w = w * ld(md, 0)
         st(MA[2], 0, w)
-        pack_rows(xa5, [(MA[2], 0)], 0)
-        pack_rows(xb5, [(MA[2], 0)], CX - 1)
+        pack_rows(xa5, [(A1[2], 0)], 0)
+        pack_rows(xb5, [(A1[2], 0)], CX - 1)
         ys5[...] = pltpu.roll(w, 11, 1)
 
     go(*r5x, *r5y)
@@ -557,11 +582,13 @@
     got(r6x, r6y, *r5x, *r5y)
     @pl.when(surface & has_xp)
     def _():
-        unpack_rows(xh5, [(MA[2], 0)], CX)
+        unpack_rows(xh5, [(A1[2], 0)], CX)
+        weigh_rows(MA, A1, (0,), CX)
 
     @pl.when(surface & has_xm)
     def _():
-        unpack_rows(xl5, [(MA[2], 0)], -1)
+        unpack_rows(xl5, [(A1[2], 0)], -1)
+        weigh_rows(MA, A1, (0,), -1)
 
     @pl.when(surface & has_yp)
     def _():
@@ -615,10 +642,14 @@
             st(A0[c], CZ, a)
             st(MA0[c], CZ, g * a)
 
-    x7 = [(ref, z) for ref in lo3 for z in (0, 1, CZ - 1)]
-    x7up = x7 + [(A0[0], z) for z in (0, 1, CZ - 1, CZ)]
+    x7 = [(ref, z) for ref in A0 for z in rim]
+    x7up = x7 + [(A0[0], CZ)]
+    ends = (0, CZ - 1)
     pack_rows(xa7, x7, 0)
     pack_rows(xb7, x7up, CX - 1)
+    for n, z in enumerate(ends):
+        xa7[16 + n:17 + n, :] = sum(row(V1[c], z, 0) * row(A1[c], z, -1) for c in range(3))
+        xb7[16 + n:17 + n, :] = sum(row(V1[c], z, CX - 1) * row(A1[c], z, CX) for c in range(3))
     r7x = [x_down(xa7, xh7), x_up(xb7, xl7)]
     go(*r7x)
     edges = (0, 1, 2, CZ - 2, CZ - 1)
@@ -629,14 +660,27 @@
 
     @pl.when(has_xp)
     def _():
-        unpack_x(xh3, lo3, CX)
+        unpack_x(xh3, A0, CX)
+        weigh_x(MA0, A0, CX)
 
     @pl.when(has_xm)
     def _():
-        unpack_x(xl3, lo3 + [A0[0]], -1)
+        unpack_x(xl3, A0, -1)
+        weigh_x(MA0, A0, -1)
 
     merge(c3, yl3, yh3)
     every(lambda z: s3(z, c3), 3, CZ - 2)
+    flat = sh.reshape(CZ * CX, CY)
+    low, high = pl.ds(0, CZ, stride=CX), pl.ds(CX - 1, CZ, stride=CX)
+
+    @pl.when(has_xp)
+    def _():
+        flat[high, :] = flat[high, :] + 0.25 * xh3[3 * CZ:, :]
+
+    @pl.when(has_xm)
+    def _():
+        flat[low, :] = flat[low, :] + 0.25 * xl3[3 * CZ:, :]
+
     pack_x(xa4, [m0], 0)
     r4x = x_down(xa4, xh4)
     go(r4x)
@@ -649,13 +693,28 @@
     @pl.when(has_xp)
     def _():
         unpack_rows(xh7, x7, CX)
+        weigh_rows(MA0, A0, rim, CX)
 
     @pl.when(has_xm)
     def _():
         unpack_rows(xl7, x7up, -1)
+        weigh_rows(MA0, A0, rim, -1)
 
     merge(c7, yl7, yh7)
     some(lambda z: s3(z, c7), edges)
+
+    def add_share(x, ends_ref, bulk_ref):
+        for z in edges:
+            at = ends_ref[16 + ends.index(z):17 + ends.index(z), :] if z in ends else bulk_ref[3 * CZ + z:3 * CZ + z + 1, :]
+            sh[z, x:x + 1, :] = sh[z, x:x + 1, :] + 0.25 * at
+
+    @pl.when(has_xp)
+    def _():
+        add_share(CX - 1, xh7, xh3)
+
+    @pl.when(has_xm)
+    def _():
+        add_share(0, xl7, xl3)
 
     @pl.when(has_zp)
     def _():
@@ -760,9 +819,9 @@
             pack, pack, pack, pack, pack, pack, pack, pack, pack, pack,
             pack, pack, pack, pack, pack, lines(24), lines(24), lines(24), lines(24), lines(8), lines(8),
             plane, plane, plane, pack, pack, pack, pack, pack, pack, pack,
-            lines(6 * CZ), lines(7 * CZ), lines(6 * CZ), lines(7 * CZ),
+            lines(7 * CZ), lines(7 * CZ), lines(7 * CZ), lines(7 * CZ),
             lines(2 * CZ), lines(2 * CZ),
-            lines(6 * CZ), lines(7 * CZ), lines(6 * CZ), lines(7 * CZ),
+            lines(4 * CZ), lines(4 * CZ), lines(4 * CZ), lines(4 * CZ),
             lines(CZ), lines(CZ),
             lines(8), lines(8), lines(8), lines(8), lines(8), lines(8),
             lines(24), lines(24), lines(24), lines(24), lines(8), lines(8),

time: 41.2 us -> 40.9 us (level)
  no operation moved by 1% of the time
where the time goes in v5:
time: 40.9 us; the launch traced here: 40.8 us
  Pallas kernels  40.1 us (98%)
  between operations  0.64 us (2%)
    pallas_call x1, Pallas kernels, shards(): pl.pallas_call(body, out_shape=(jax.ShapeDtypeStruct((3, CZ, CX, CY), F32...  39 us
    pallas_call x1, Pallas kernels, shards(): pl.pallas_call(hand_out, out_shape=[jax.ShapeDtypeStruct(a.shape, F32) fo...  1.09 us

profile of v5, /device:TPU:1, one launch (start us, length us, event | category | flops | bytes accessed | tf_op | source)
XLA Modules:
  0.0 40.8 jit_solution(16002138997184115385)
XLA Ops:
  0.6 39.0 %adjoint.1 = (f32[3,32,16,128]{3,2,1,0:T(8,128)S(1)}, f32[32,16,128]{2,1,0:T(8,128)S(1)}, f32[32,16,128]{2,1,0:T(8,128)S(1)}) custom-call(f32[3,32,16,128]{3,2,1,0:T(8,128)} %vel.1, f32[32,16,128]{2,1,0:T(8,128)} %pres.1, f32[32,16,128]{2,1,0:T(8,128)} %modulus.1, f32[3,32,16,128]{3,2,1,0:T(8,128)} %avel.1, f32[32,16,128]{2,1,0:T(8,128)} %apres.1, ...), custom_call_target="tpu_custom_call" | custom-call | flops 20000000 | bytes 3670016 | tf_op jit(solution)/shard_map/adjoint/pallas_call | solution.py:807
  39.7 1.1 %handout.1 = (f32[3,32,16,128]{3,2,1,0:T(8,128)}, f32[32,16,128]{2,1,0:T(8,128)}, f32[32,16,128]{2,1,0:T(8,128)}) custom-call(f32[3,32,16,128]{3,2,1,0:T(8,128)S(1)} %get-tuple-element.6.a, f32[32,16,128]{2,1,0:T(8,128)S(1)} %get-tuple-element.7.b, f32[32,16,128]{2,1,0:T(8,128)S(1)} %get-tuple-element.8.c), custom_call_target="tpu_custom_call" | custom-call | tf_op jit(solution)/shard_map/handout/pallas_call | solution.py:843

commit v6 on v5

--- a/solution.py
+++ b/solution.py
@@ -326,6 +326,13 @@
     def go(*those):
         for one in those:
             one.start()
+
+    settled = []
+
+    def settle(*those):
+        for one in those:
+            one.flush()
+            settled.append(one)
 
     def got(*those):
         for one in those:
@@ -578,6 +585,9 @@
     pack_layers(ys6, [p1, m1, A1[2]], rim)
     r6y = y_down(ys6, yh6)
     go(r6y)
+    settle(*r9x, *r1y, *r1x, *zraw, r10x, r9y, r2x, r2y)
+    for copy in stage1 + stage2:
+        copy.wait_send()
 
     got(r6x, r6y, *r5x, *r5y)
     @pl.when(surface & has_xp)
@@ -738,6 +748,7 @@
 
     every(lambda z: s4(z, yh4), 3, CZ - 3)
     early = store(3, CZ - 6, 0)
+    settle(*r3x, *r3y, *r5x, *r5y, r6x, r6y, *r7x, *r7y)
     got(r8x, r8y)
 
     @pl.when(has_xp)
@@ -757,10 +768,8 @@
 
     late = store(0, 3, 1) + store(CZ - 3, 3, 2)
     for one in links:
-        if one not in zpart and one not in zpm:
+        if one not in zpart + zpm + settled:
             one.flush()
-    for copy in stage1 + stage2:
-        copy.wait_send()
 
     @pl.when(gz > 0)
     def _():

time: 40.9 us -> 40.8 us (level)
  no operation moved by 1% of the time
where the time goes in v6:
time: 40.8 us; the launch traced here: 40.7 us
  Pallas kernels  40.1 us (98%)
  between operations  0.64 us (2%)
    pallas_call x1, Pallas kernels, shards(): pl.pallas_call(body, out_shape=(jax.ShapeDtypeStruct((3, CZ, CX, CY), F32...  39 us
    pallas_call x1, Pallas kernels, shards(): pl.pallas_call(hand_out, out_shape=[jax.ShapeDtypeStruct(a.shape, F32) fo...  1.09 us

profile of v6, /device:TPU:1, one launch (start us, length us, event | category | flops | bytes accessed | tf_op | source)
XLA Modules:
  0.0 40.7 jit_solution(5624266018153347158)
XLA Ops:
  0.6 39.0 %adjoint.1 = (f32[3,32,16,128]{3,2,1,0:T(8,128)S(1)}, f32[32,16,128]{2,1,0:T(8,128)S(1)}, f32[32,16,128]{2,1,0:T(8,128)S(1)}) custom-call(f32[3,32,16,128]{3,2,1,0:T(8,128)} %vel.1, f32[32,16,128]{2,1,0:T(8,128)} %pres.1, f32[32,16,128]{2,1,0:T(8,128)} %modulus.1, f32[3,32,16,128]{3,2,1,0:T(8,128)} %avel.1, f32[32,16,128]{2,1,0:T(8,128)} %apres.1, ...), custom_call_target="tpu_custom_call" | custom-call | flops 20000000 | bytes 3670016 | tf_op jit(solution)/shard_map/adjoint/pallas_call | solution.py:816
  39.6 1.1 %handout.1 = (f32[3,32,16,128]{3,2,1,0:T(8,128)}, f32[32,16,128]{2,1,0:T(8,128)}, f32[32,16,128]{2,1,0:T(8,128)}) custom-call(f32[3,32,16,128]{3,2,1,0:T(8,128)S(1)} %get-tuple-element.6.a, f32[32,16,128]{2,1,0:T(8,128)S(1)} %get-tuple-element.7.b, f32[32,16,128]{2,1,0:T(8,128)S(1)} %get-tuple-element.8.c), custom_call_target="tpu_custom_call" | custom-call | tf_op jit(solution)/shard_map/handout/pallas_call | solution.py:852
